TPU v7x, 32 devices: a whole 2x2x4 slice. The times are simulated.
32 devices in a mesh: win: 2 (over x), sub: 16 (over z, y, core).
Axes of the slice: x: 2, y: 2, z: 4, core: 2. Of those that a mesh axis runs over, the one named last changes fastest.
Arguments:
- pulses: bfloat16 [32, 80, 2, 4096], P(('win', 'sub')), parts along dimension 0, may hold values from -6 to 6
- offsets: int32 [32, 80], P(('win', 'sub')), parts along dimension 0, may hold values from 0 to 3968
- geometry: float32 [32, 3, 80], P(('win', 'sub')), parts along dimension 0, may hold values from -1 to 1
- counts: int32 [32], P(('win', 'sub')), parts along dimension 0, may hold values from 48 to 80, as said below
Outputs:
- frames: float32 [32, 2, 32, 512], P(('win', 'sub')), parts along dimension 0
- cumulative: float32 [32, 2, 32, 512], P(('win', 'sub')), parts along dimension 0
There are 2 independent parts, one for each index of `win`. A program takes and returns all parts, laid end to end along the dimension named above; each array names one. Nothing has to cross between parts.
Inputs may be any that keep to these rules, and one draw needn't show every extreme that they name: Subaperture s holds its pulses in slots 0 to counts[s] - 1; the other slots are unused. Some subaperture has 80 pulses and some 48.
All inputs are finite; a program needn't handle non-finite values.
Results may differ from a plain program's by a relative error of at most 0.004.
Values sent between devices are 32-bit elements; how exact they have to be, the bound alone decides.
No kernel may reach another device: no remote copies, remote signals or barrier semaphores. Data moves between devices by JAX's collectives and lax.ppermute only.
A program may use at most 192 MiB of HBM per device.

v0:
```python
import math

import jax
import jax.numpy as jnp
from jax import lax
from jax.sharding import PartitionSpec as P

ROWS = 32
COLS = 512
BINS = 128


def spectrum_of(pulse_rows, vertical_offset_along, geometry_sub, count, width):
    slots = pulse_rows.shape[0]
    windows = jax.vmap(lambda one_row, offset: lax.dynamic_slice_in_dim(one_row, offset, width, 1))(
        pulse_rows, vertical_offset_along
    ).astype(jnp.float32)
    index = jnp.arange(width, dtype=jnp.int32)
    shifted = index - width // 2
    turns = index[:, None] * shifted[None, :] % width
    angle = 2.0 * math.pi / width * turns.astype(jnp.float32)
    cosine = jnp.cos(angle)
    sine = jnp.sin(angle)
    highest = lax.Precision.HIGHEST
    real_in = windows[:, 0]
    imag_in = windows[:, 1]
    real_out = (
        jnp.dot(real_in, cosine, precision=highest) + jnp.dot(imag_in, sine, precision=highest)
    ) / width
    imag_out = (
        jnp.dot(imag_in, cosine, precision=highest) - jnp.dot(real_in, sine, precision=highest)
    ) / width
    viewing_bearing = 2.0 * math.pi * (shifted.astype(jnp.float32) / width + 0.37)
    scene_middle = width / 2.0 + width / 16.0 * geometry_sub[0]
    radar_frequency = 2.0 * math.pi / 100.0 * (37 * vertical_offset_along % 100).astype(jnp.float32)
    signal_argument = viewing_bearing[None, :] * scene_middle[:, None] + radar_frequency[:, None]
    live = (jnp.arange(slots, dtype=jnp.int32) < count).astype(jnp.float32) / math.sqrt(slots)
    cos_phase = jnp.cos(signal_argument)
    sin_phase = jnp.sin(signal_argument)
    coefficient_real = live[:, None] * (real_out * cos_phase - imag_out * sin_phase)
    coef_im = live[:, None] * (real_out * sin_phase + imag_out * cos_phase)
    return (coefficient_real, coef_im, viewing_bearing)


def block_product(
    coefficient_real, coef_im, viewing_bearing, row_slope, column_gradient, rows, cols
):
    xpos = (jnp.arange(rows, dtype=jnp.int32) - rows // 2).astype(jnp.float32)
    ypos = (jnp.arange(cols, dtype=jnp.int32) - cols // 2).astype(jnp.float32)
    angle_x = xpos[:, None, None] * (viewing_bearing[None, :] * row_slope[:, None])[None]
    cosine_x = jnp.cos(angle_x)
    sine_x = jnp.sin(angle_x)
    left_re = coefficient_real[None] * cosine_x - coef_im[None] * sine_x
    left_im = coefficient_real[None] * sine_x + coef_im[None] * cosine_x
    left = jnp.concatenate([left_re.reshape(rows, -1), left_im.reshape(rows, -1)], axis=1).astype(
        jnp.bfloat16
    )
    angle_y = (viewing_bearing[None, :] * column_gradient[:, None])[:, :, None] * ypos[
        None, None, :
    ]
    right_re = jnp.cos(angle_y).reshape(-1, cols)
    right_im = jnp.sin(angle_y).reshape(-1, cols)
    upper = jnp.concatenate([right_re, right_im], axis=1)
    lower = jnp.concatenate([-right_im, right_re], axis=1)
    right = jnp.concatenate([upper, lower], axis=0).astype(jnp.bfloat16)
    return jnp.dot(left, right, preferred_element_type=jnp.float32)


def shards(pulses, offsets, geometry, counts):
    rows = ROWS
    cols = COLS
    width = BINS
    slots = pulses.shape[1]
    count = counts[0]
    geometry_sub = geometry[0]
    coefficient_real, coef_im, viewing_bearing = spectrum_of(
        pulses[0], offsets[0], geometry_sub, count, width
    )
    row_slope = 0.05 * geometry_sub[1]
    column_gradient = 0.05 * geometry_sub[2]

    def add_block(step, total):
        start = (step * 8).astype(jnp.int32)
        part_re = lax.dynamic_slice_in_dim(coefficient_real, start, 8, 0)
        part_im = lax.dynamic_slice_in_dim(coef_im, start, 8, 0)
        slope_r = lax.dynamic_slice_in_dim(row_slope, start, 8, 0)
        slope_c = lax.dynamic_slice_in_dim(column_gradient, start, 8, 0)
        return total + block_product(
            part_re, part_im, viewing_bearing, slope_r, slope_c, rows, cols
        )

    empty = jnp.zeros((rows, 2 * cols), jnp.float32)
    total = lax.fori_loop(0, slots // 8, add_block, empty)
    own = jnp.stack([total[:, :cols], total[:, cols:]], axis=0)[None]
    flattened = own.reshape(1, 2 * rows * cols)
    by_pixels = lax.all_to_all(flattened, "sub", split_axis=1, concat_axis=0, tiled=True)
    members = by_pixels.shape[0]
    running = jnp.cumsum(by_pixels, axis=0)
    delayed = jnp.concatenate([jnp.zeros((8, running.shape[1]), jnp.float32), running[:-8]], axis=0)
    frame_rows = (running - delayed) / math.sqrt(8.0)
    magnitude_factor = jnp.sqrt(jnp.arange(1, members + 1, dtype=jnp.int32).astype(jnp.float32))
    cumulative_rows = running / magnitude_factor[:, None]
    frames_back, cumulative_back = (
        lax.all_to_all(frame_rows, "sub", split_axis=0, concat_axis=1, tiled=True),
        lax.all_to_all(cumulative_rows, "sub", split_axis=0, concat_axis=1, tiled=True),
    )
    frames = frames_back.reshape(1, 2, rows, cols)
    cumulative = cumulative_back.reshape(1, 2, rows, cols)
    return (frames, cumulative)


def solution(mesh):
    return jax.shard_map(
        shards,
        mesh=mesh,
        in_specs=(
            P(("win", "sub"), None, None, None),
            P(("win", "sub"), None),
            P(("win", "sub"), None, None),
            P(("win", "sub")),
        ),
        out_specs=(P(("win", "sub"), None, None, None), P(("win", "sub"), None, None, None)),
        check_vma=False,
    )
```

profile of v0, /device:TPU:0, one launch (start us, length us, event | category | flops | bytes accessed | tf_op | source)
XLA Modules:
  0.0 226.3 jit_solution(11494692594200224226)
XLA Ops:
  0.7 56.8 %copy.10 = bf16[1,80,2,4096]{2,1,3,0:T(8,128)(2,1)} copy(bf16[1,80,2,4096]{3,2,1,0:T(2,128)(2,1)} %param.6) | data formatting | bytes 2621440 | tf_op args[0]
  57.5 17.8 %gather_fusion = bf16[80,2,128]{1,0,2:T(8,128)(2,1)S(1)} fusion(bf16[80,2,4096]{1,0,2:T(8,128)(2,1)} %bitcast.1, s32[80]{0:T(128)S(1)} %fusion.56), kind=kCustom, calls=%fused_computation | custom fusion | bytes 82880 | tf_op jit(solution)/shard_map/vmap()/gather | solution.py:15
  75.2 3.2 %fusion.73 = (bf16[80,1,128]{1,0,2:T(8,128)(2,1)}, bf16[80,1,128]{1,0,2:T(8,128)(2,1)}) fusion(bf16[80,2,128]{1,0,2:T(8,128)(2,1)S(1)} %gather_fusion), kind=kLoop, calls=%fused_computation.101 | loop fusion | bytes 81920 | tf_op jit(solution)/shard_map/slice | solution.py:25
  78.4 3.1 %copy.11 = bf16[80,1,128]{2,0,1:T(8,128)(2,1)S(1)} copy(bf16[80,1,128]{1,0,2:T(8,128)(2,1)} %get-tuple-element.243) | data formatting | bytes 40960 | tf_op jit(solution)/shard_map/slice | solution.py:25
  81.5 1.6 copy.12
  85.5 100.0 %while.17 = (s32[]{:T(128)}, f32[32,1024]{1,0:T(8,128)S(1)}, f32[80,128]{1,0:T(8,128)S(1)}, f32[80]{0:T(128)S(1)}, f32[80,128]{1,0:T(8,128)S(1)}, /*index=5*/f32...) while((s32[]{:T(128)}, f32[32,1024]{1,0:T(8,128)S(1)}, ...), condition=%wide.region_1.2_spmd.clone.clone, body=%wide.region_0.1_spmd.clone.clone.sunk | while | flops 154242752 | bytes 6879337 | solution.py:93
  86.7 8.2 %fusion.81 = (bf16[1024,512]{1,0:T(8,128)(2,1)S(1)}, bf16[1024,512]{1,0:T(8,128)(2,1)S(1)}, bf16[1024,512]{1,0:T(8,128)(2,1)S(1)}) fusion(f32[512]{0:T(512)S(1)} %add_convert_fusion.4, f32[1024]{0:T(1024)S(1)} %bitcast_multiply_fusion.4), kind=kLoop, calls=%fused_computation.13.clone.1 | loop fusion | flops 2621440 | bytes 3151872 | tf_op jit(solution)/shard_map/convert.5
  94.9 0.8 fusion.83
  96.6 8.2 %fusion.81 = (bf16[1024,512]{1,0:T(8,128)(2,1)S(1)}, bf16[1024,512]{1,0:T(8,128)(2,1)S(1)}, bf16[1024,512]{1,0:T(8,128)(2,1)S(1)}) fusion(f32[512]{0:T(512)S(1)} %add_convert_fusion.4, f32[1024]{0:T(1024)S(1)} %bitcast_multiply_fusion.4), kind=kLoop, calls=%fused_computation.13.clone.1 | loop fusion | flops 2621440 | bytes 3151872 | tf_op jit(solution)/shard_map/convert.5
  106.6 8.2 %fusion.81 = (bf16[1024,512]{1,0:T(8,128)(2,1)S(1)}, bf16[1024,512]{1,0:T(8,128)(2,1)S(1)}, bf16[1024,512]{1,0:T(8,128)(2,1)S(1)}) fusion(f32[512]{0:T(512)S(1)} %add_convert_fusion.4, f32[1024]{0:T(1024)S(1)} %bitcast_multiply_fusion.4), kind=kLoop, calls=%fused_computation.13.clone.1 | loop fusion | flops 2621440 | bytes 3151872 | tf_op jit(solution)/shard_map/convert.5
  116.6 8.2 %fusion.81 = (bf16[1024,512]{1,0:T(8,128)(2,1)S(1)}, bf16[1024,512]{1,0:T(8,128)(2,1)S(1)}, bf16[1024,512]{1,0:T(8,128)(2,1)S(1)}) fusion(f32[512]{0:T(512)S(1)} %add_convert_fusion.4, f32[1024]{0:T(1024)S(1)} %bitcast_multiply_fusion.4), kind=kLoop, calls=%fused_computation.13.clone.1 | loop fusion | flops 2621440 | bytes 3151872 | tf_op jit(solution)/shard_map/convert.5
  126.6 8.2 %fusion.81 = (bf16[1024,512]{1,0:T(8,128)(2,1)S(1)}, bf16[1024,512]{1,0:T(8,128)(2,1)S(1)}, bf16[1024,512]{1,0:T(8,128)(2,1)S(1)}) fusion(f32[512]{0:T(512)S(1)} %add_convert_fusion.4, f32[1024]{0:T(1024)S(1)} %bitcast_multiply_fusion.4), kind=kLoop, calls=%fused_computation.13.clone.1 | loop fusion | flops 2621440 | bytes 3151872 | tf_op jit(solution)/shard_map/convert.5
  136.5 8.2 %fusion.81 = (bf16[1024,512]{1,0:T(8,128)(2,1)S(1)}, bf16[1024,512]{1,0:T(8,128)(2,1)S(1)}, bf16[1024,512]{1,0:T(8,128)(2,1)S(1)}) fusion(f32[512]{0:T(512)S(1)} %add_convert_fusion.4, f32[1024]{0:T(1024)S(1)} %bitcast_multiply_fusion.4), kind=kLoop, calls=%fused_computation.13.clone.1 | loop fusion | flops 2621440 | bytes 3151872 | tf_op jit(solution)/shard_map/convert.5
  146.5 8.2 %fusion.81 = (bf16[1024,512]{1,0:T(8,128)(2,1)S(1)}, bf16[1024,512]{1,0:T(8,128)(2,1)S(1)}, bf16[1024,512]{1,0:T(8,128)(2,1)S(1)}) fusion(f32[512]{0:T(512)S(1)} %add_convert_fusion.4, f32[1024]{0:T(1024)S(1)} %bitcast_multiply_fusion.4), kind=kLoop, calls=%fused_computation.13.clone.1 | loop fusion | flops 2621440 | bytes 3151872 | tf_op jit(solution)/shard_map/convert.5
  156.5 8.2 %fusion.81 = (bf16[1024,512]{1,0:T(8,128)(2,1)S(1)}, bf16[1024,512]{1,0:T(8,128)(2,1)S(1)}, bf16[1024,512]{1,0:T(8,128)(2,1)S(1)}) fusion(f32[512]{0:T(512)S(1)} %add_convert_fusion.4, f32[1024]{0:T(1024)S(1)} %bitcast_multiply_fusion.4), kind=kLoop, calls=%fused_computation.13.clone.1 | loop fusion | flops 2621440 | bytes 3151872 | tf_op jit(solution)/shard_map/convert.5
  166.5 8.2 %fusion.81 = (bf16[1024,512]{1,0:T(8,128)(2,1)S(1)}, bf16[1024,512]{1,0:T(8,128)(2,1)S(1)}, bf16[1024,512]{1,0:T(8,128)(2,1)S(1)}) fusion(f32[512]{0:T(512)S(1)} %add_convert_fusion.4, f32[1024]{0:T(1024)S(1)} %bitcast_multiply_fusion.4), kind=kLoop, calls=%fused_computation.13.clone.1 | loop fusion | flops 2621440 | bytes 3151872 | tf_op jit(solution)/shard_map/convert.5
  176.5 8.2 %fusion.81 = (bf16[1024,512]{1,0:T(8,128)(2,1)S(1)}, bf16[1024,512]{1,0:T(8,128)(2,1)S(1)}, bf16[1024,512]{1,0:T(8,128)(2,1)S(1)}) fusion(f32[512]{0:T(512)S(1)} %add_convert_fusion.4, f32[1024]{0:T(1024)S(1)} %bitcast_multiply_fusion.4), kind=kLoop, calls=%fused_computation.13.clone.1 | loop fusion | flops 2621440 | bytes 3151872 | tf_op jit(solution)/shard_map/convert.5
  185.5 0.8 all_to_all.30
  186.4 7.2 %all-to-all-start = ((f32[1,16,2048]{2,0,1:T(1,128)}), f32[1,16,2048]{2,0,1:T(1,128)S(1)}, u32[]{:S(2)}, u32[]{:S(2)}) async-start(f32[1,16,2048]{2,0,1:T(1,128)} %all_to_all.30), calls=%async_computation | async-start | bytes 262144 | tf_op jit(solution)/shard_map/all_to_all | solution.py:96
  193.5 7.9 %all-to-all-done = f32[1,16,2048]{2,0,1:T(1,128)S(1)} async-done(((f32[1,16,2048]{2,0,1:T(1,128)}), f32[1,16,2048]{2,0,1:T(1,128)S(1)}, u32[]{:S(2)}, u32[]{:S(2)}) %all-to-all-start) | async-done | bytes 131104 | tf_op jit(solution)/shard_map/all_to_all | solution.py:96
  202.5 3.5 %all-to-all-start.1 = ((f32[16,1,2048]{2,1,0:T(1,128)}), f32[16,1,2048]{2,1,0:T(1,128)S(1)}, u32[]{:S(2)}, u32[]{:S(2)}) async-start(f32[16,1,2048]{2,1,0:T(1,128)} %copy.13), calls=%async_computation.1 | async-start | bytes 262144 | tf_op jit(solution)/shard_map/all_to_all | solution.py:104
  206.9 7.0 %all-to-all-done.1 = f32[16,1,2048]{2,1,0:T(1,128)S(1)} async-done(((f32[16,1,2048]{2,1,0:T(1,128)}), f32[16,1,2048]{2,1,0:T(1,128)S(1)}, u32[]{:S(2)}, u32[]{:S(2)}) %all-to-all-start.1) | async-done | bytes 131104 | tf_op jit(solution)/shard_map/all_to_all | solution.py:104
  213.9 3.5 %all-to-all-start.2 = ((f32[16,1,2048]{2,1,0:T(1,128)}), f32[16,1,2048]{2,1,0:T(1,128)S(1)}, u32[]{:S(2)}, u32[]{:S(2)}) async-start(f32[16,1,2048]{2,1,0:T(1,128)} %copy.14), calls=%async_computation.2 | async-start | bytes 262144 | tf_op jit(solution)/shard_map/all_to_all | solution.py:105
  218.4 6.9 %all-to-all-done.2 = f32[16,1,2048]{2,1,0:T(1,128)S(1)} async-done(((f32[16,1,2048]{2,1,0:T(1,128)}), f32[16,1,2048]{2,1,0:T(1,128)S(1)}, u32[]{:S(2)}, u32[]{:S(2)}) %all-to-all-start.2) | async-done | bytes 131104 | tf_op jit(solution)/shard_map/all_to_all | solution.py:105
  (149 shorter events, 21.8 us)
Async XLA Ops:
  0.7 56.8 %copy-start.2 = (s32[1,80]{1,0:T(1,128)S(1)}, s32[1,80]{1,0:T(1,128)}, u32[]{:S(2)}) copy-start(s32[1,80]{1,0:T(1,128)} %param.7) | copy-start | bytes 964
  78.4 3.1 %copy-start = (bf16[80,1,128]{1,0,2:T(8,128)(2,1)S(1)}, bf16[80,1,128]{1,0,2:T(8,128)(2,1)}, u32[]{:S(2)}) copy-start(bf16[80,1,128]{1,0,2:T(8,128)(2,1)} %get-tuple-element.244) | copy-start | bytes 61444
  78.4 6.0 %copy-start.1 = (f32[1,3,80]{2,0,1:T(1,128)S(1)}, f32[1,3,80]{2,0,1:T(1,128)}, u32[]{:S(2)}) copy-start(f32[1,3,80]{2,0,1:T(1,128)} %param.8) | copy-start | bytes 2884
  186.4 15.1 %all-to-all-start = ((f32[1,16,2048]{2,0,1:T(1,128)}), f32[1,16,2048]{2,0,1:T(1,128)S(1)}, u32[]{:S(2)}, u32[]{:S(2)}) async-start(f32[1,16,2048]{2,0,1:T(1,128)} %all_to_all.30), calls=%async_computation | async-start | bytes 262144 | tf_op jit(solution)/shard_map/all_to_all | solution.py:96
  202.5 11.4 %all-to-all-start.1 = ((f32[16,1,2048]{2,1,0:T(1,128)}), f32[16,1,2048]{2,1,0:T(1,128)S(1)}, u32[]{:S(2)}, u32[]{:S(2)}) async-start(f32[16,1,2048]{2,1,0:T(1,128)} %copy.13), calls=%async_computation.1 | async-start | bytes 262144 | tf_op jit(solution)/shard_map/all_to_all | solution.py:104
  213.9 11.4 %all-to-all-start.2 = ((f32[16,1,2048]{2,1,0:T(1,128)}), f32[16,1,2048]{2,1,0:T(1,128)S(1)}, u32[]{:S(2)}, u32[]{:S(2)}) async-start(f32[16,1,2048]{2,1,0:T(1,128)} %copy.14), calls=%async_computation.2 | async-start | bytes 262144 | tf_op jit(solution)/shard_map/all_to_all | solution.py:105
where the time goes:
time: 228 us; the launch traced here: 226 us
  other arithmetic  89.6 us (39%)
  local copies, waits for them, and re-layouts  88.7 us (39%)
  waiting for transfers between devices  21.8 us (10%)
  starting transfers between devices  14.2 us (6%)
  matrix products  9.69 us (4%)
    another operation x20, other arithmetic  87.8 us
    unnamed x8, local copies, waits for them, and re-layouts  56.8 us
    gather x1, local copies, waits for them, and re-layouts, spectrum_of(): lax.dynamic_slice_in_dim(one_row, offset, width, 1)  17.8 us
    dot_general x10, matrix products, block_product(): return jnp.dot(left, right, preferred_element_type=jnp.float32)  7.96 us
    all_to_all x1, waiting for transfers between devices, shards(): lax.all_to_all(flattened, 'sub', split_axis=1, concat_axis=0, tiled=True)  7.92 us
    all_to_all x1, starting transfers between devices, shards(): lax.all_to_all(flattened, 'sub', split_axis=1, concat_axis=0, tiled=True)  7.16 us
    all_to_all x1, waiting for transfers between devices, shards(): lax.all_to_all(frame_rows, 'sub', split_axis=0, concat_axis=1, tiled=True)  7.03 us
    all_to_all x1, waiting for transfers between devices, shards(): lax.all_to_all(cumulative_rows, 'sub', split_axis=0, concat_axis=1, tiled...  6.89 us
  transfers between devices with their start and end apart: 3, of which 3 were waited for; matrix products, arithmetic and copies ran while one was open for 1% of the time, Pallas kernels for 0%

commit v1 on v0

v1 whole, which is shorter than its diff:
```python
import functools
import math

import jax
import jax.numpy as jnp
from jax import lax
from jax.experimental import pallas as pl
from jax.experimental.pallas import tpu as pltpu
from jax.sharding import PartitionSpec as P

ROWS = 32
COLS = 512
BINS = 128
WINDOW = 8
LANES = 128
GROUP = 8

SIN = (3.141592580044369, -5.167706878903419, 2.5500313768938527, -0.5980451717629565, 0.07722012423151481)
COS = (0.999999953468687, -4.934792858755703, 4.0584119149345526, -1.3318801632613946, 0.21969679848706386)


def horner(coefficients, u):
    total = jnp.full_like(u, coefficients[-1])
    for c in coefficients[-2::-1]:
        total = total * u + c
    return total


def cis_turns(turns):
    f = turns - jnp.round(turns)
    u = f * f
    s = f * horner(SIN, u)
    c = horner(COS, u)
    return 1.0 - 2.0 * s * s, 2.0 * s * c


def cmul(a, b):
    return a[0] * b[0] - a[1] * b[1], a[0] * b[1] + a[1] * b[0]


def csquare(a):
    return a[0] * a[0] - a[1] * a[1], 2.0 * a[0] * a[1]


def image_kernel(rows, cols, width, counts_s, offsets_s, offsets_v, geometry_v, pulses_any, out_ref,
                 held, window_f32, columns, seeds, steps, acc, sem):
    slots, _, samples = held.shape
    pieces = cols // LANES
    load = pltpu.make_async_copy(pulses_any.at[0], held, sem)
    load.start()

    columns[...] = jnp.zeros_like(columns)
    columns[0:3, 0:slots] = geometry_v[0]
    columns[3:4, 0:slots] = offsets_v[...].astype(jnp.float32)
    by_pulse = jnp.transpose(columns[...])[0:slots]
    geo_centre = by_pulse[:, 0:1]
    slope_r = 0.05 * by_pulse[:, 1:2]
    slope_c = 0.05 * by_pulse[:, 2:3]
    offset = by_pulse[:, 3:4]
    shape = (slots, LANES)
    lane = lax.broadcasted_iota(jnp.int32, shape, 1).astype(jnp.float32)
    g = lane - width // 2
    theta = g / width + 0.37
    y_local = lane
    last_block = samples // LANES - 2
    block = jnp.minimum(jnp.floor(offset / LANES), last_block)
    rest = offset - LANES * block

    angle = slope_c * y_local
    base = cis_turns(angle * (0.37 - (width // 2) / width))
    one = cis_turns(angle / width)
    now = base
    for r in range(8):
        for k in range(2):
            seeds[2 + k, pl.ds(r, slots, stride=8), :] = now[k]
        if r < 7:
            now = cmul(now, one)
    ratio = csquare(csquare(csquare(one)))
    for level in range(4):
        for k in range(2):
            steps[8 + 2 * level + k] = ratio[k]
        ratio = csquare(ratio)

    row_one = cis_turns(theta * slope_r)
    ratio = csquare(csquare(csquare(row_one)))
    piece = cis_turns(theta * (slope_c * LANES))
    for level, value in enumerate((ratio, csquare(ratio), piece, csquare(piece))):
        for k in range(2):
            steps[2 * level + k] = value[k]

    b_index = lax.broadcasted_iota(jnp.int32, (width, width), 0).astype(jnp.float32)
    g_index = lax.broadcasted_iota(jnp.int32, (width, width), 1).astype(jnp.float32) - width // 2
    cosine, sine = cis_turns(b_index * g_index / width)
    fourier = jnp.concatenate(
        [jnp.concatenate([cosine, -sine], axis=1), jnp.concatenate([sine, cosine], axis=1)], axis=0
    )
    fourier_high = fourier.astype(jnp.bfloat16)
    fourier_low = (fourier - fourier_high.astype(jnp.float32)).astype(jnp.bfloat16)

    phase = theta * ((width / 2.0 + width / 16.0 * geo_centre) - slope_r * (rows // 2) - slope_c * (cols // 2))
    scaled = 37.0 * offset
    steps37 = (scaled - 100.0 * jnp.round(scaled / 100.0)) / 100.0
    circular = g * rest / width
    phase = phase + (circular - jnp.round(circular)) + steps37
    phase_cis = cis_turns(phase)

    load.wait()
    for p in range(slots):
        start = jnp.minimum(offsets_s[0, p] // LANES, last_block) * LANES
        pair = held[p, :, pl.ds(pl.multiple_of(start, LANES), 2 * LANES)].astype(jnp.float32)
        for half in range(2):
            window_f32[half, 2 * p:2 * p + 2, :] = pair[:, half * LANES:(half + 1) * LANES]
    in_first = lane >= rest
    parts = []
    for k in range(2):
        first = window_f32[0, pl.ds(k, slots, stride=2), :]
        second = window_f32[1, pl.ds(k, slots, stride=2), :]
        parts.append(jnp.where(in_first, first, second))
    folded = jnp.concatenate(parts, axis=1).astype(jnp.bfloat16)
    spectrum = jnp.dot(folded, fourier_high, preferred_element_type=jnp.float32) + jnp.dot(
        folded, fourier_low, preferred_element_type=jnp.float32
    )
    live = lax.broadcasted_iota(jnp.int32, shape, 0) < counts_s[0]
    scale = jnp.where(live, 1.0 / (width * math.sqrt(slots)), 0.0)
    now = cmul((spectrum[:, 0:LANES] * scale, spectrum[:, LANES:] * scale), phase_cis)
    for r in range(8):
        for k in range(2):
            seeds[k, pl.ds(r, slots, stride=8), :] = now[k]
        if r < 7:
            now = cmul(now, row_one)

    acc[...] = jnp.zeros_like(acc)

    def grown(seed, first_step, pulse):
        values = [seed]
        for level in range(4):
            step = tuple(
                jnp.broadcast_to(steps[first_step + 2 * level + k, pl.ds(pulse, 1), :], (8, LANES)) for k in range(2)
            )
            values = values + [cmul(v, step) for v in values]
        return [jnp.concatenate([v[k] for v in values], axis=0) for k in range(2)]

    def add_group(step, carry):
        lefts = []
        rights = []
        for i in range(GROUP):
            pulse = step * GROUP + i
            at = pl.ds(pl.multiple_of(8 * pulse, 8), 8)
            left = grown((seeds[0, at, :], seeds[1, at, :]), 0, pulse)
            lefts += [v.astype(jnp.bfloat16) for v in left]
            right_re, right_im = grown((seeds[2, at, :], seeds[3, at, :]), 8, pulse)
            rights.append(jnp.concatenate([right_re, right_im], axis=1).astype(jnp.bfloat16))
            rights.append(jnp.concatenate([-right_im, right_re], axis=1).astype(jnp.bfloat16))
        acc[...] += jnp.dot(
            jnp.concatenate(lefts, axis=1), jnp.concatenate(rights, axis=0), preferred_element_type=jnp.float32
        )
        return carry

    lax.fori_loop(0, slots // GROUP, add_group, 0)
    for piece_at in range(pieces):
        for k in range(2):
            out_ref[0, k, :, piece_at * LANES:(piece_at + 1) * LANES] = acc[
                piece_at * rows:(piece_at + 1) * rows, k * LANES:(k + 1) * LANES
            ]


def image_of(pulses, offsets, geometry, counts):
    _, slots, _, samples = pulses.shape
    vmem = pl.BlockSpec(memory_space=pltpu.VMEM)
    smem = pl.BlockSpec(memory_space=pltpu.SMEM)
    return pl.pallas_call(
        functools.partial(image_kernel, ROWS, COLS, BINS),
        out_shape=jax.ShapeDtypeStruct((1, 2, ROWS, COLS), jnp.float32),
        in_specs=[smem, smem, vmem, vmem, pl.BlockSpec(memory_space=pl.ANY)],
        out_specs=vmem,
        scratch_shapes=[
            pltpu.VMEM((slots, 2, samples), pulses.dtype),
            pltpu.VMEM((2, 2 * slots, LANES), jnp.float32),
            pltpu.VMEM((LANES, LANES), jnp.float32),
            pltpu.VMEM((4, 8 * slots, LANES), jnp.float32),
            pltpu.VMEM((16, slots, LANES), jnp.float32),
            pltpu.VMEM((COLS // LANES * ROWS, 2 * LANES), jnp.float32),
            pltpu.SemaphoreType.DMA(()),
        ],
        compiler_params=pltpu.CompilerParams(vmem_limit_bytes=40 * 1024 * 1024),
    )(counts, offsets, offsets, geometry, pulses)


def shards(pulses, offsets, geometry, counts):
    image = image_of(pulses, offsets, geometry, counts)
    members = lax.axis_size("sub")
    me = lax.axis_index("sub")
    position = me % WINDOW

    def exchange(value, distance):
        return lax.ppermute(value, "sub", [(i, i ^ distance) for i in range(members)])

    upto = image
    after = jnp.zeros_like(image)
    distance = 1
    while distance < min(WINDOW, members):
        other = exchange(upto + after, distance)
        upper = (me & distance) != 0
        upto = jnp.where(upper, upto + other, upto)
        after = jnp.where(upper, after, after + other)
        distance *= 2
    total = upto + after
    lagged = lax.ppermute(after, "sub", [(i, i + WINDOW) for i in range(members - WINDOW)])
    prefix = upto
    while distance < members:
        other = exchange(total, distance)
        upper = (me & distance) != 0
        prefix = jnp.where(upper, prefix + other, prefix)
        total = total + other
        distance *= 2
    frames = (upto + lagged) * (1.0 / math.sqrt(WINDOW))
    cumulative = prefix / jnp.sqrt((me + 1).astype(jnp.float32))
    return frames, cumulative


def solution(mesh):
    return jax.shard_map(
        shards,
        mesh=mesh,
        in_specs=(
            P(("win", "sub"), None, None, None),
            P(("win", "sub"), None),
            P(("win", "sub"), None, None),
            P(("win", "sub")),
        ),
        out_specs=(P(("win", "sub"), None, None, None), P(("win", "sub"), None, None, None)),
        check_vma=False,
    )
```

time: 228 us -> 38 us (0.17)
  the two profiles are of different devices: /device:TPU:0 before, /device:TPU:25 now
where the time goes in v1:
time: 38 us; the launch traced here: 37.8 us
  waiting for transfers between devices  20.2 us (53%)
  starting transfers between devices  6.63 us (17%)
  Pallas kernels  6.02 us (16%)
  local copies, waits for them, and re-layouts  2.65 us (7%)
  between operations  1.38 us (4%)
  other arithmetic  0.84 us (2%)
    ppermute x4, waiting for transfers between devices, exchange(): lax.ppermute(value, 'sub', [(i, i ^ distance) for i in range(members)])  10.9 us
    ppermute x1, waiting for transfers between devices, shards(): lax.ppermute(after, 'sub', [(i, i + WINDOW) for i in range(members - WIND...  9.31 us
    pallas_call x1, Pallas kernels, image_of(): pl.pallas_call(functools.partial(image_kernel, ROWS, COLS, BINS), out_sha...  6.02 us
    ppermute x4, starting transfers between devices, exchange(): lax.ppermute(value, 'sub', [(i, i ^ distance) for i in range(members)])  5.33 us
    unnamed x5, local copies, waits for them, and re-layouts  2.65 us
    ppermute x1, starting transfers between devices, shards(): lax.ppermute(after, 'sub', [(i, i + WINDOW) for i in range(members - WIND...  1.29 us
  transfers between devices with their start and end apart: 5, of which 5 were waited for; matrix products, arithmetic and copies ran while one was open for 0% of the time, Pallas kernels for 0%

profile of v1, /device:TPU:25, one launch (start us, length us, event | category | flops | bytes accessed | tf_op | source)
XLA Modules:
  0.0 37.8 jit_solution(7991420627885143310)
XLA Ops:
  0.6 0.7 %copy.6.geometry_v = f32[1,3,80]{2,1,0:T(4,128)S(1)} copy(f32[1,3,80]{2,0,1:T(1,128)} %param.6) | data formatting | bytes 1920 | tf_op args[2]
  2.0 0.0 copy-start
  2.0 1.3 %copy-done = bf16[1,80,2,4096]{3,2,1,0:T(2,128)(2,1)S(1)} copy-done((bf16[1,80,2,4096]{3,2,1,0:T(2,128)(2,1)S(1)}, bf16[1,80,2,4096]{3,2,1,0:T(2,128)(2,1)}, u32[]{:S(2)}) %copy-start) | copy-done | bytes 1310744
  3.3 0.0 copy-start.1
  3.3 0.7 %copy-done.1 = s32[1,80]{1,0:T(1,128)S(1)} copy-done((s32[1,80]{1,0:T(1,128)S(1)}, s32[1,80]{1,0:T(1,128)}, u32[]{:S(2)}) %copy-start.1) | copy-done | bytes 344
  3.9 6.0 %shard_map.59 = f32[1,2,32,512]{3,2,1,0:T(8,128)S(1)} custom-call(s32[1]{0:T(128)S(6)} %copy.7.counts_s, s32[1,80]{1,0:T(1,128)S(1)} %copy-done.1, s32[1,80]{1,0:T(1,128)S(1)} %copy-done.1, f32[1,3,80]{2,1,0:T(4,128)S(1)} %copy.6.geometry_v, bf16[1,80,2,4096]{3,2,1,0:T(2,128)(2,1)S(1)} %copy-done), custom_call_target="tpu_custom_call" | custom-call | tf_op jit(solution)/shard_map/pallas_call | solution.py:171
  10.0 0.7 %collective-permute-start = (f32[1,2,32,512]{3,2,1,0:T(8,128)S(1)}, f32[1,2,32,512]{3,2,1,0:T(8,128)S(1)}, u32[]{:S(2)}, u32[]{:S(2)}) collective-permute-start(f32[1,2,32,512]{3,2,1,0:T(8,128)S(1)} %shard_map.59), channel_id=1, source_target_pairs={{0,1},{1,0},{2,3},{3,2},{4,5},{5,4},{6,7},{7,6},{8,9},{9,8},{10,11... | collective-permute-start | bytes 393224 | tf_op jit(solution)/shard_map/ppermute | solution.py:196
  10.7 1.0 %collective-permute-done = f32[1,2,32,512]{3,2,1,0:T(8,128)S(1)} collective-permute-done((f32[1,2,32,512]{3,2,1,0:T(8,128)S(1)}, f32[1,2,32,512]{3,2,1,0:T(8,128)S(1)}, u32[]{:S(2)}, u32[]{:S(2)}) %collective-permute-start) | collective-permute-done | bytes 131104 | tf_op jit(solution)/shard_map/ppermute | solution.py:196
  11.7 1.3 %collective-permute-start.1 = (f32[1,2,32,512]{3,2,1,0:T(8,128)S(1)}, f32[1,2,32,512]{3,2,1,0:T(8,128)S(1)}, u32[]{:S(2)}, u32[]{:S(2)}) collective-permute-start(f32[1,2,32,512]{3,2,1,0:T(8,128)S(1)} %select_add_fusion), channel_id=1, source_target_pairs={{0,2},{1,3},{2,0},{3,1},{4,6},{5,7},{6,4},{7,5},{8,10},{9,11},{10,... | collective-permute-start | bytes 393224 | tf_op jit(solution)/shard_map/ppermute | solution.py:196
  13.0 3.5 %collective-permute-done.1 = f32[1,2,32,512]{3,2,1,0:T(8,128)S(1)} collective-permute-done((f32[1,2,32,512]{3,2,1,0:T(8,128)S(1)}, f32[1,2,32,512]{3,2,1,0:T(8,128)S(1)}, u32[]{:S(2)}, u32[]{:S(2)}) %collective-permute-start.1) | collective-permute-done | bytes 131104 | tf_op jit(solution)/shard_map/ppermute | solution.py:196
  16.6 0.2 collective-permute-start.2
  16.8 3.6 %collective-permute-done.2 = f32[1,2,32,512]{3,2,1,0:T(8,128)S(1)} collective-permute-done((f32[1,2,32,512]{3,2,1,0:T(8,128)S(1)}, f32[1,2,32,512]{3,2,1,0:T(8,128)S(1)}, u32[]{:S(2)}, u32[]{:S(2)}) %collective-permute-start.2) | collective-permute-done | bytes 131104 | tf_op jit(solution)/shard_map/ppermute | solution.py:196
  20.5 1.3 %collective-permute-start.3 = (f32[1,2,32,512]{3,2,1,0:T(8,128)S(1)}, f32[1,2,32,512]{3,2,1,0:T(8,128)S(1)}, u32[]{:S(2)}, u32[]{:S(2)}) collective-permute-start(f32[1,2,32,512]{3,2,1,0:T(8,128)S(1)} %get-tuple-element.3), channel_id=1, source_target_pairs={{0,8},{1,9},{2,10},{3,11},{4,12},{5,13},{6,14},{7,15},{16,24},{17,... | collective-permute-start | bytes 393224 | tf_op jit(solution)/shard_map/ppermute | solution.py:208
  21.8 3.0 %collective-permute-start.4 = (f32[1,2,32,512]{3,2,1,0:T(8,128)S(1)}, f32[1,2,32,512]{3,2,1,0:T(8,128)S(1)}, u32[]{:S(2)}, u32[]{:S(2)}) collective-permute-start(f32[1,2,32,512]{3,2,1,0:T(8,128)S(1)} %get-tuple-element.2), channel_id=1, source_target_pairs={{0,8},{1,9},{2,10},{3,11},{4,12},{5,13},{6,14},{7,15},{8,0},{9,1},... | collective-permute-start | bytes 393224 | tf_op jit(solution)/shard_map/ppermute | solution.py:196
  24.9 9.3 %collective-permute-done.3 = f32[1,2,32,512]{3,2,1,0:T(8,128)S(1)} collective-permute-done((f32[1,2,32,512]{3,2,1,0:T(8,128)S(1)}, f32[1,2,32,512]{3,2,1,0:T(8,128)S(1)}, u32[]{:S(2)}, u32[]{:S(2)}) %collective-permute-start.3) | collective-permute-done | bytes 131104 | tf_op jit(solution)/shard_map/ppermute | solution.py:208
  34.2 2.8 %collective-permute-done.4 = f32[1,2,32,512]{3,2,1,0:T(8,128)S(1)} collective-permute-done((f32[1,2,32,512]{3,2,1,0:T(8,128)S(1)}, f32[1,2,32,512]{3,2,1,0:T(8,128)S(1)}, u32[]{:S(2)}, u32[]{:S(2)}) %collective-permute-start.4) | collective-permute-done | bytes 131104 | tf_op jit(solution)/shard_map/ppermute | solution.py:196
  37.0 0.7 %fusion = (f32[1,2,32,512]{3,2,1,0:T(8,128)}, f32[1,2,32,512]{3,2,1,0:T(8,128)}) fusion(f32[1,2,32,512]{3,2,1,0:T(8,128)S(1)} %get-tuple-element.4, f32[1,2,32,512]{3,2,1,0:T(8,128)S(1)} %collective-permute-done.4, f32[]{:T(128)S(6)} %sqrt.3, pred[]{:T(512)S(6)} %ne.15, f32[1,2,32,512]{3,2,1,0:T(8,128)S(1)} %collective-permute-done.3), kind=kLoop, calls=%fused_computation.6 | loop fusion | flops 163840 | bytes 655365 | tf_op jit(solution)/shard_map/div | solution.py:217
  (3 shorter events, 0.1 us)
Async XLA Ops:
  2.0 1.3 %copy-start = (bf16[1,80,2,4096]{3,2,1,0:T(2,128)(2,1)S(1)}, bf16[1,80,2,4096]{3,2,1,0:T(2,128)(2,1)}, u32[]{:S(2)}) copy-start(bf16[1,80,2,4096]{3,2,1,0:T(2,128)(2,1)} %pulses_any.1) | copy-start | bytes 3932164
  3.3 0.7 %copy-start.1 = (s32[1,80]{1,0:T(1,128)S(1)}, s32[1,80]{1,0:T(1,128)}, u32[]{:S(2)}) copy-start(s32[1,80]{1,0:T(1,128)} %offsets_v.1) | copy-start | bytes 964
  10.0 1.7 %collective-permute-start = (f32[1,2,32,512]{3,2,1,0:T(8,128)S(1)}, f32[1,2,32,512]{3,2,1,0:T(8,128)S(1)}, u32[]{:S(2)}, u32[]{:S(2)}) collective-permute-start(f32[1,2,32,512]{3,2,1,0:T(8,128)S(1)} %shard_map.59), channel_id=1, source_target_pairs={{0,1},{1,0},{2,3},{3,2},{4,5},{5,4},{6,7},{7,6},{8,9},{9,8},{10,11... | collective-permute-start | bytes 393224 | tf_op jit(solution)/shard_map/ppermute | solution.py:196
  11.7 4.8 %collective-permute-start.1 = (f32[1,2,32,512]{3,2,1,0:T(8,128)S(1)}, f32[1,2,32,512]{3,2,1,0:T(8,128)S(1)}, u32[]{:S(2)}, u32[]{:S(2)}) collective-permute-start(f32[1,2,32,512]{3,2,1,0:T(8,128)S(1)} %select_add_fusion), channel_id=1, source_target_pairs={{0,2},{1,3},{2,0},{3,1},{4,6},{5,7},{6,4},{7,5},{8,10},{9,11},{10,... | collective-permute-start | bytes 393224 | tf_op jit(solution)/shard_map/ppermute | solution.py:196
  16.6 3.9 %collective-permute-start.2 = (f32[1,2,32,512]{3,2,1,0:T(8,128)S(1)}, f32[1,2,32,512]{3,2,1,0:T(8,128)S(1)}, u32[]{:S(2)}, u32[]{:S(2)}) collective-permute-start(f32[1,2,32,512]{3,2,1,0:T(8,128)S(1)} %get-tuple-element.5), channel_id=1, source_target_pairs={{0,4},{1,5},{2,6},{3,7},{4,0},{5,1},{6,2},{7,3},{8,12},{9,13},{10,... | collective-permute-start | bytes 393224 | tf_op jit(solution)/shard_map/ppermute | solution.py:196
  20.5 13.7 %collective-permute-start.3 = (f32[1,2,32,512]{3,2,1,0:T(8,128)S(1)}, f32[1,2,32,512]{3,2,1,0:T(8,128)S(1)}, u32[]{:S(2)}, u32[]{:S(2)}) collective-permute-start(f32[1,2,32,512]{3,2,1,0:T(8,128)S(1)} %get-tuple-element.3), channel_id=1, source_target_pairs={{0,8},{1,9},{2,10},{3,11},{4,12},{5,13},{6,14},{7,15},{16,24},{17,... | collective-permute-start | bytes 393224 | tf_op jit(solution)/shard_map/ppermute | solution.py:208
  21.8 15.2 %collective-permute-start.4 = (f32[1,2,32,512]{3,2,1,0:T(8,128)S(1)}, f32[1,2,32,512]{3,2,1,0:T(8,128)S(1)}, u32[]{:S(2)}, u32[]{:S(2)}) collective-permute-start(f32[1,2,32,512]{3,2,1,0:T(8,128)S(1)} %get-tuple-element.2), channel_id=1, source_target_pairs={{0,8},{1,9},{2,10},{3,11},{4,12},{5,13},{6,14},{7,15},{8,0},{9,1},... | collective-permute-start | bytes 393224 | tf_op jit(solution)/shard_map/ppermute | solution.py:196

commit v2 on v1

--- a/solution.py
+++ b/solution.py
@@ -42,7 +42,7 @@
     return a[0] * a[0] - a[1] * a[1], 2.0 * a[0] * a[1]
 
 
-def image_kernel(rows, cols, width, counts_s, offsets_s, offsets_v, geometry_v, pulses_any, out_ref,
+def image_kernel(rows, cols, width, counts_s, offsets_s, offsets_v, geometry_v, pulses_any, kept_ref, sent_ref,
                  held, window_f32, columns, seeds, steps, acc, sem):
     slots, _, samples = held.shape
     pieces = cols // LANES
@@ -157,22 +157,24 @@
         return carry
 
     lax.fori_loop(0, slots // GROUP, add_group, 0)
+    second = lax.rem(lax.axis_index("sub"), 2) == 1
     for piece_at in range(pieces):
-        for k in range(2):
-            out_ref[0, k, :, piece_at * LANES:(piece_at + 1) * LANES] = acc[
-                piece_at * rows:(piece_at + 1) * rows, k * LANES:(k + 1) * LANES
-            ]
-
-
-def image_of(pulses, offsets, geometry, counts):
+        at = slice(piece_at * rows, (piece_at + 1) * rows)
+        real, imag = acc[at, 0:LANES], acc[at, LANES:2 * LANES]
+        lanes = slice(piece_at * LANES, (piece_at + 1) * LANES)
+        kept_ref[:, lanes] = jnp.where(second, imag, real)
+        sent_ref[:, lanes] = jnp.where(second, real, imag)
+
+
+def halves_of_image(pulses, offsets, geometry, counts):
     _, slots, _, samples = pulses.shape
     vmem = pl.BlockSpec(memory_space=pltpu.VMEM)
     smem = pl.BlockSpec(memory_space=pltpu.SMEM)
     return pl.pallas_call(
         functools.partial(image_kernel, ROWS, COLS, BINS),
-        out_shape=jax.ShapeDtypeStruct((1, 2, ROWS, COLS), jnp.float32),
+        out_shape=[jax.ShapeDtypeStruct((ROWS, COLS), jnp.float32)] * 2,
         in_specs=[smem, smem, vmem, vmem, pl.BlockSpec(memory_space=pl.ANY)],
-        out_specs=vmem,
+        out_specs=[vmem, vmem],
         scratch_shapes=[
             pltpu.VMEM((slots, 2, samples), pulses.dtype),
             pltpu.VMEM((2, 2 * slots, LANES), jnp.float32),
@@ -187,35 +189,65 @@
 
 
 def shards(pulses, offsets, geometry, counts):
-    image = image_of(pulses, offsets, geometry, counts)
     members = lax.axis_size("sub")
     me = lax.axis_index("sub")
-    position = me % WINDOW
-
-    def exchange(value, distance):
+    kept, sent = halves_of_image(pulses, offsets, geometry, counts)
+
+    def swap(value, distance):
         return lax.ppermute(value, "sub", [(i, i ^ distance) for i in range(members)])
 
-    upto = image
-    after = jnp.zeros_like(image)
-    distance = 1
-    while distance < min(WINDOW, members):
-        other = exchange(upto + after, distance)
-        upper = (me & distance) != 0
-        upto = jnp.where(upper, upto + other, upto)
-        after = jnp.where(upper, after, after + other)
-        distance *= 2
-    total = upto + after
-    lagged = lax.ppermute(after, "sub", [(i, i + WINDOW) for i in range(members - WINDOW)])
-    prefix = upto
-    while distance < members:
-        other = exchange(total, distance)
-        upper = (me & distance) != 0
-        prefix = jnp.where(upper, prefix + other, prefix)
-        total = total + other
-        distance *= 2
-    frames = (upto + lagged) * (1.0 / math.sqrt(WINDOW))
-    cumulative = prefix / jnp.sqrt((me + 1).astype(jnp.float32))
-    return frames, cumulative
+    def ahead(value, distance):
+        return lax.ppermute(value, "sub", [(i, i + distance) for i in range(members - distance)])
+
+    odd = me % 2 == 1
+    upper = me // 2 % 2 == 1
+    block = me // 4
+    blocks = members // 4
+    got = swap(sent, 1)
+    first = jnp.where(odd, got, kept)
+    second = jnp.where(odd, kept, got)
+    pair = first + second
+
+    if blocks <= 4:
+        nothing = jnp.zeros_like(pair)
+        earlier = last = before_last = oldest = nothing
+        for k in range(1, blocks):
+            value = jnp.stack([pair, second]) if k == 2 else pair
+            value = swap(value, 4 * k)
+            if k == 2:
+                oldest = jnp.where(block >= 2, value[1], nothing)
+                value = value[0]
+                before_last = jnp.where(block >= 2, value, nothing)
+            source = block ^ k
+            earlier = earlier + jnp.where(source < block, value, nothing)
+            last = last + jnp.where(source == block - 1, value, nothing)
+    else:
+        last = ahead(pair, 4)
+        before_last, oldest = ahead(jnp.stack([pair, second]), 8)
+        earlier = last
+        distance = 4
+        while distance < members:
+            earlier = earlier + ahead(earlier, distance)
+            distance *= 2
+
+    mine = jnp.stack([
+        earlier + jnp.where(upper, 0.0, pair),
+        last + jnp.where(upper, before_last, pair),
+    ])
+    other = swap(mine, 2)
+    earlier = earlier + other[0]
+    recent = last + other[1]
+    frame_scale = 1.0 / math.sqrt(WINDOW)
+    number = (me - me % 2 + 1).astype(jnp.float32)
+    firsts = jnp.stack([(first + recent + oldest) * frame_scale, (earlier + first) / jnp.sqrt(number)])
+    seconds = jnp.stack([(pair + recent) * frame_scale, (earlier + pair) / jnp.sqrt(number + 1.0)])
+
+    own = jnp.where(odd, seconds, firsts)
+    back = swap(jnp.where(odd, firsts, seconds), 1)
+    real = jnp.where(odd, back, own)
+    imag = jnp.where(odd, own, back)
+    frames, cumulative = jnp.stack([real, imag], axis=1)
+    return frames[None], cumulative[None]
 
 
 def solution(mesh):

time: 38 us -> 31.8 us (0.84)
  the two profiles are of different devices: /device:TPU:25 before, /device:TPU:0 now
where the time goes in v2:
time: 31.8 us; the launch traced here: 31.3 us
  waiting for transfers between devices  12.3 us (39%)
  starting transfers between devices  8.04 us (25%)
  Pallas kernels  6.03 us (19%)
  local copies, waits for them, and re-layouts  2.65 us (8%)
  between operations  1.43 us (4%)
  other arithmetic  0.88 us (3%)
    ppermute x6, waiting for transfers between devices, swap(): lax.ppermute(value, 'sub', [(i, i ^ distance) for i in range(members)])  12.3 us
    ppermute x6, starting transfers between devices, swap(): lax.ppermute(value, 'sub', [(i, i ^ distance) for i in range(members)])  8.04 us
    pallas_call x1, Pallas kernels, halves_of_image(): pl.pallas_call(functools.partial(image_kernel, ROWS, COLS, BINS), out_sha...  6.03 us
    unnamed x5, local copies, waits for them, and re-layouts  2.65 us
    unnamed x1, other arithmetic  0.72 us
  transfers between devices with their start and end apart: 6, of which 6 were waited for; matrix products, arithmetic and copies ran while one was open for 0% of the time, Pallas kernels for 0%

profile of v2, /device:TPU:0, one launch (start us, length us, event | category | flops | bytes accessed | tf_op | source)
XLA Modules:
  0.0 31.3 jit_solution(6314341770199550801)
XLA Ops:
  1.3 0.7 %copy.6.geometry_v = f32[1,3,80]{2,1,0:T(4,128)S(1)} copy(f32[1,3,80]{2,0,1:T(1,128)} %param.6) | data formatting | bytes 1920 | tf_op args[2]
  2.0 0.0 copy-start
  2.0 1.3 %copy-done = bf16[1,80,2,4096]{3,2,1,0:T(2,128)(2,1)S(1)} copy-done((bf16[1,80,2,4096]{3,2,1,0:T(2,128)(2,1)S(1)}, bf16[1,80,2,4096]{3,2,1,0:T(2,128)(2,1)}, u32[]{:S(2)}) %copy-start) | copy-done | bytes 1310744
  3.3 0.0 copy-start.1
  3.3 0.7 %copy-done.1 = s32[1,80]{1,0:T(1,128)S(1)} copy-done((s32[1,80]{1,0:T(1,128)S(1)}, s32[1,80]{1,0:T(1,128)}, u32[]{:S(2)}) %copy-start.1) | copy-done | bytes 344
  3.9 6.0 %shard_map.59 = (f32[32,512]{1,0:T(8,128)S(1)}, f32[32,512]{1,0:T(8,128)S(1)}) custom-call(s32[1]{0:T(128)S(6)} %copy.9.counts_s, s32[1,80]{1,0:T(1,128)S(1)} %copy-done.1, s32[1,80]{1,0:T(1,128)S(1)} %copy-done.1, f32[1,3,80]{2,1,0:T(4,128)S(1)} %copy.6.geometry_v, bf16[1,80,2,4096]{3,2,1,0:T(2,128)(2,1)S(1)} %copy-done), custom_call_target="tpu_custom_call" | custom-call | tf_op jit(solution)/shard_map/pallas_call | solution.py:173
  10.0 0.5 %collective-permute-start = (f32[32,512]{1,0:T(8,128)S(1)}, f32[32,512]{1,0:T(8,128)S(1)}, u32[]{:S(2)}, u32[]{:S(2)}) collective-permute-start(f32[32,512]{1,0:T(8,128)S(1)} %get-tuple-element.4), channel_id=1, source_target_pairs={{0,1},{1,0},{2,3},{3,2},{4,5},{5,4},{6,7},{7,6},{8,9},{9,8},{10,11... | collective-permute-start | bytes 196616 | tf_op jit(solution)/shard_map/ppermute | solution.py:197
  10.5 0.9 %collective-permute-done = f32[32,512]{1,0:T(8,128)S(1)} collective-permute-done((f32[32,512]{1,0:T(8,128)S(1)}, f32[32,512]{1,0:T(8,128)S(1)}, u32[]{:S(2)}, u32[]{:S(2)}) %collective-permute-start) | collective-permute-done | bytes 65568 | tf_op jit(solution)/shard_map/ppermute | solution.py:197
  11.4 4.0 %collective-permute-start.2 = (f32[2,32,512]{2,1,0:T(8,128)S(1)}, f32[2,32,512]{2,1,0:T(8,128)S(1)}, u32[]{:S(2)}, u32[]{:S(2)}) collective-permute-start(f32[2,32,512]{2,1,0:T(8,128)S(1)} %pad_maximum_fusion.1), channel_id=1, source_target_pairs={{0,8},{1,9},{2,10},{3,11},{4,12},{5,13},{6,14},{7,15},{8,0},{9,1},... | collective-permute-start | bytes 393224 | tf_op jit(solution)/shard_map/ppermute | solution.py:197
  15.4 1.3 %collective-permute-start.3 = (f32[32,512]{1,0:T(8,128)S(1)}, f32[32,512]{1,0:T(8,128)S(1)}, u32[]{:S(2)}, u32[]{:S(2)}) collective-permute-start(f32[32,512]{1,0:T(8,128)S(1)} %get-tuple-element.12), channel_id=1, source_target_pairs={{0,12},{1,13},{2,14},{3,15},{4,8},{5,9},{6,10},{7,11},{8,4},{9,5},... | collective-permute-start | bytes 196616 | tf_op jit(solution)/shard_map/ppermute | solution.py:197
  16.8 0.2 collective-permute-start.1
  17.0 5.4 %collective-permute-done.3 = f32[32,512]{1,0:T(8,128)S(1)} collective-permute-done((f32[32,512]{1,0:T(8,128)S(1)}, f32[32,512]{1,0:T(8,128)S(1)}, u32[]{:S(2)}, u32[]{:S(2)}) %collective-permute-start.3) | collective-permute-done | bytes 65568 | tf_op jit(solution)/shard_map/ppermute | solution.py:197
  22.4 1.3 %collective-permute-done.1 = f32[32,512]{1,0:T(8,128)S(1)} collective-permute-done((f32[32,512]{1,0:T(8,128)S(1)}, f32[32,512]{1,0:T(8,128)S(1)}, u32[]{:S(2)}, u32[]{:S(2)}) %collective-permute-start.1) | collective-permute-done | bytes 65568 | tf_op jit(solution)/shard_map/ppermute | solution.py:197
  23.7 0.3 collective-permute-done.2
  24.0 1.9 %collective-permute-start.4 = (f32[2,32,512]{2,1,0:T(8,128)S(1)}, f32[2,32,512]{2,1,0:T(8,128)S(1)}, u32[]{:S(2)}, u32[]{:S(2)}) collective-permute-start(f32[2,32,512]{2,1,0:T(8,128)S(1)} %pad_maximum_fusion.2), channel_id=1, source_target_pairs={{0,2},{1,3},{2,0},{3,1},{4,6},{5,7},{6,4},{7,5},{8,10},{9,11},{10,... | collective-permute-start | bytes 393224 | tf_op jit(solution)/shard_map/ppermute | solution.py:197
  26.0 3.1 %collective-permute-done.4 = f32[2,32,512]{2,1,0:T(8,128)S(1)} collective-permute-done((f32[2,32,512]{2,1,0:T(8,128)S(1)}, f32[2,32,512]{2,1,0:T(8,128)S(1)}, u32[]{:S(2)}, u32[]{:S(2)}) %collective-permute-start.4) | collective-permute-done | bytes 131104 | tf_op jit(solution)/shard_map/ppermute | solution.py:197
  29.1 0.1 collective-permute-start.5
  29.2 1.3 %collective-permute-done.5 = f32[2,32,512]{2,1,0:T(8,128)S(1)} collective-permute-done((f32[2,32,512]{2,1,0:T(8,128)S(1)}, f32[2,32,512]{2,1,0:T(8,128)S(1)}, u32[]{:S(2)}, u32[]{:S(2)}) %collective-permute-start.5) | collective-permute-done | bytes 131104 | tf_op jit(solution)/shard_map/ppermute | solution.py:197
  30.6 0.7 %fusion.2 = (f32[1,2,32,512]{3,2,1,0:T(8,128)}, f32[1,2,32,512]{3,2,1,0:T(8,128)}) fusion(f32[2,1,32,512]{3,2,0,1:T(8,128)S(1)} %get-tuple-element.14, f32[2,1,32,512]{3,2,0,1:T(8,128)S(1)} %get-tuple-element.15), kind=kLoop, calls=%fused_computation.5 | loop fusion | flops 65536 | bytes 524288
  (7 shorter events, 0.2 us)
Async XLA Ops:
  2.0 1.3 %copy-start = (bf16[1,80,2,4096]{3,2,1,0:T(2,128)(2,1)S(1)}, bf16[1,80,2,4096]{3,2,1,0:T(2,128)(2,1)}, u32[]{:S(2)}) copy-start(bf16[1,80,2,4096]{3,2,1,0:T(2,128)(2,1)} %pulses_any.1) | copy-start | bytes 3932164
  3.3 0.7 %copy-start.1 = (s32[1,80]{1,0:T(1,128)S(1)}, s32[1,80]{1,0:T(1,128)}, u32[]{:S(2)}) copy-start(s32[1,80]{1,0:T(1,128)} %offsets_v.1) | copy-start | bytes 964
  10.0 1.4 %collective-permute-start = (f32[32,512]{1,0:T(8,128)S(1)}, f32[32,512]{1,0:T(8,128)S(1)}, u32[]{:S(2)}, u32[]{:S(2)}) collective-permute-start(f32[32,512]{1,0:T(8,128)S(1)} %get-tuple-element.4), channel_id=1, source_target_pairs={{0,1},{1,0},{2,3},{3,2},{4,5},{5,4},{6,7},{7,6},{8,9},{9,8},{10,11... | collective-permute-start | bytes 196616 | tf_op jit(solution)/shard_map/ppermute | solution.py:197
  11.4 12.5 %collective-permute-start.2 = (f32[2,32,512]{2,1,0:T(8,128)S(1)}, f32[2,32,512]{2,1,0:T(8,128)S(1)}, u32[]{:S(2)}, u32[]{:S(2)}) collective-permute-start(f32[2,32,512]{2,1,0:T(8,128)S(1)} %pad_maximum_fusion.1), channel_id=1, source_target_pairs={{0,8},{1,9},{2,10},{3,11},{4,12},{5,13},{6,14},{7,15},{8,0},{9,1},... | collective-permute-start | bytes 393224 | tf_op jit(solution)/shard_map/ppermute | solution.py:197
  15.4 7.0 %collective-permute-start.3 = (f32[32,512]{1,0:T(8,128)S(1)}, f32[32,512]{1,0:T(8,128)S(1)}, u32[]{:S(2)}, u32[]{:S(2)}) collective-permute-start(f32[32,512]{1,0:T(8,128)S(1)} %get-tuple-element.12), channel_id=1, source_target_pairs={{0,12},{1,13},{2,14},{3,15},{4,8},{5,9},{6,10},{7,11},{8,4},{9,5},... | collective-permute-start | bytes 196616 | tf_op jit(solution)/shard_map/ppermute | solution.py:197
  16.8 6.9 %collective-permute-start.1 = (f32[32,512]{1,0:T(8,128)S(1)}, f32[32,512]{1,0:T(8,128)S(1)}, u32[]{:S(2)}, u32[]{:S(2)}) collective-permute-start(f32[32,512]{1,0:T(8,128)S(1)} %get-tuple-element.12), channel_id=1, source_target_pairs={{0,4},{1,5},{2,6},{3,7},{4,0},{5,1},{6,2},{7,3},{8,12},{9,13},{10,... | collective-permute-start | bytes 196616 | tf_op jit(solution)/shard_map/ppermute | solution.py:197
  24.0 5.0 %collective-permute-start.4 = (f32[2,32,512]{2,1,0:T(8,128)S(1)}, f32[2,32,512]{2,1,0:T(8,128)S(1)}, u32[]{:S(2)}, u32[]{:S(2)}) collective-permute-start(f32[2,32,512]{2,1,0:T(8,128)S(1)} %pad_maximum_fusion.2), channel_id=1, source_target_pairs={{0,2},{1,3},{2,0},{3,1},{4,6},{5,7},{6,4},{7,5},{8,10},{9,11},{10,... | collective-permute-start | bytes 393224 | tf_op jit(solution)/shard_map/ppermute | solution.py:197
  29.1 1.4 %collective-permute-start.5 = (f32[2,32,512]{2,1,0:T(8,128)S(1)}, f32[2,32,512]{2,1,0:T(8,128)S(1)}, u32[]{:S(2)}, u32[]{:S(2)}) collective-permute-start(f32[2,32,512]{2,1,0:T(8,128)S(1)} %fusion.4), channel_id=1, source_target_pairs={{0,1},{1,0},{2,3},{3,2},{4,5},{5,4},{6,7},{7,6},{8,9},{9,8},{10,11... | collective-permute-start | bytes 393224 | tf_op jit(solution)/shard_map/ppermute | solution.py:197

commit v3 on v2

--- a/solution.py
+++ b/solution.py
@@ -42,15 +42,35 @@
     return a[0] * a[0] - a[1] * a[1], 2.0 * a[0] * a[1]
 
 
-def image_kernel(rows, cols, width, counts_s, offsets_s, offsets_v, geometry_v, pulses_any, kept_ref, sent_ref,
-                 held, window_f32, columns, seeds, steps, acc, sem):
+def image_kernel(rows, cols, width, counts_s, offsets_h, geometry_h, pulses_h, kept_ref, sent_ref,
+                 held, window_f32, geometry_v, offsets_v, offsets_s, columns, seeds, steps, acc, sems):
     slots, _, samples = held.shape
     pieces = cols // LANES
-    load = pltpu.make_async_copy(pulses_any.at[0], held, sem)
+    small = [
+        pltpu.make_async_copy(source, target, sems.at[k])
+        for k, (source, target) in enumerate((
+            (geometry_h, geometry_v), (offsets_h, offsets_v), (offsets_h, offsets_s),
+        ))
+    ]
+    for copy in small:
+        copy.start()
+    load = pltpu.make_async_copy(pulses_h.at[0], held, sems.at[3])
     load.start()
 
+    b_index = lax.broadcasted_iota(jnp.int32, (width, width), 0).astype(jnp.float32)
+    g_index = lax.broadcasted_iota(jnp.int32, (width, width), 1).astype(jnp.float32) - width // 2
+    cosine, sine = cis_turns(b_index * g_index / width)
+    fourier = jnp.concatenate(
+        [jnp.concatenate([cosine, -sine], axis=1), jnp.concatenate([sine, cosine], axis=1)], axis=0
+    )
+    fourier_high = fourier.astype(jnp.bfloat16)
+    fourier_low = (fourier - fourier_high.astype(jnp.float32)).astype(jnp.bfloat16)
+
     columns[...] = jnp.zeros_like(columns)
-    columns[0:3, 0:slots] = geometry_v[0]
+    for copy in small:
+        copy.wait()
+    for k in range(3):
+        columns[k:k + 1, 0:slots] = geometry_v[k]
     columns[3:4, 0:slots] = offsets_v[...].astype(jnp.float32)
     by_pulse = jnp.transpose(columns[...])[0:slots]
     geo_centre = by_pulse[:, 0:1]
@@ -87,15 +107,6 @@
     for level, value in enumerate((ratio, csquare(ratio), piece, csquare(piece))):
         for k in range(2):
             steps[2 * level + k] = value[k]
-
-    b_index = lax.broadcasted_iota(jnp.int32, (width, width), 0).astype(jnp.float32)
-    g_index = lax.broadcasted_iota(jnp.int32, (width, width), 1).astype(jnp.float32) - width // 2
-    cosine, sine = cis_turns(b_index * g_index / width)
-    fourier = jnp.concatenate(
-        [jnp.concatenate([cosine, -sine], axis=1), jnp.concatenate([sine, cosine], axis=1)], axis=0
-    )
-    fourier_high = fourier.astype(jnp.bfloat16)
-    fourier_low = (fourier - fourier_high.astype(jnp.float32)).astype(jnp.bfloat16)
 
     phase = theta * ((width / 2.0 + width / 16.0 * geo_centre) - slope_r * (rows // 2) - slope_c * (cols // 2))
     scaled = 37.0 * offset
@@ -169,23 +180,27 @@
 def halves_of_image(pulses, offsets, geometry, counts):
     _, slots, _, samples = pulses.shape
     vmem = pl.BlockSpec(memory_space=pltpu.VMEM)
-    smem = pl.BlockSpec(memory_space=pltpu.SMEM)
+    hbm = pl.BlockSpec(memory_space=pltpu.HBM)
+    held = (offsets, jnp.transpose(geometry, (1, 0, 2)), pulses)
     return pl.pallas_call(
         functools.partial(image_kernel, ROWS, COLS, BINS),
         out_shape=[jax.ShapeDtypeStruct((ROWS, COLS), jnp.float32)] * 2,
-        in_specs=[smem, smem, vmem, vmem, pl.BlockSpec(memory_space=pl.ANY)],
+        in_specs=[pl.BlockSpec(memory_space=pltpu.SMEM), hbm, hbm, hbm],
         out_specs=[vmem, vmem],
         scratch_shapes=[
             pltpu.VMEM((slots, 2, samples), pulses.dtype),
             pltpu.VMEM((2, 2 * slots, LANES), jnp.float32),
+            pltpu.VMEM((3, 1, slots), jnp.float32),
+            pltpu.VMEM((1, slots), jnp.int32),
+            pltpu.SMEM((1, slots), jnp.int32),
             pltpu.VMEM((LANES, LANES), jnp.float32),
             pltpu.VMEM((4, 8 * slots, LANES), jnp.float32),
             pltpu.VMEM((16, slots, LANES), jnp.float32),
             pltpu.VMEM((COLS // LANES * ROWS, 2 * LANES), jnp.float32),
-            pltpu.SemaphoreType.DMA(()),
+            pltpu.SemaphoreType.DMA((4,)),
         ],
         compiler_params=pltpu.CompilerParams(vmem_limit_bytes=40 * 1024 * 1024),
-    )(counts, offsets, offsets, geometry, pulses)
+    )(counts, *(pltpu.with_memory_space_constraint(x, pltpu.HBM) for x in held))
 
 
 def shards(pulses, offsets, geometry, counts):

time: 31.8 us -> 29.4 us (0.925)
  local copies, waits for them, and re-layouts: 2.65 us -> 0 us
    unnamed x5 -> x0, local copies, waits for them, and re-layouts: 2.65 us -> none
where the time goes in v3:
time: 29.4 us; the launch traced here: 28.9 us
  waiting for transfers between devices  12.3 us (42%)
  starting transfers between devices  8.04 us (27%)
  Pallas kernels  6.25 us (21%)
  between operations  1.43 us (5%)
  other arithmetic  0.88 us (3%)
    ppermute x6, waiting for transfers between devices, swap(): lax.ppermute(value, 'sub', [(i, i ^ distance) for i in range(members)])  12.3 us
    ppermute x6, starting transfers between devices, swap(): lax.ppermute(value, 'sub', [(i, i ^ distance) for i in range(members)])  8.04 us
    pallas_call x1, Pallas kernels, halves_of_image(): pl.pallas_call(functools.partial(image_kernel, ROWS, COLS, BINS), out_sha...  6.25 us
    unnamed x1, other arithmetic  0.72 us
  transfers between devices with their start and end apart: 6, of which 6 were waited for; matrix products, arithmetic and copies ran while one was open for 0% of the time, Pallas kernels for 0%

profile of v3, /device:TPU:0, one launch (start us, length us, event | category | flops | bytes accessed | tf_op | source)
XLA Modules:
  0.0 28.9 jit_solution(4509628810853610722)
XLA Ops:
  1.3 6.3 %shard_map.59 = (f32[32,512]{1,0:T(8,128)S(1)}, f32[32,512]{1,0:T(8,128)S(1)}) custom-call(s32[1]{0:T(128)S(6)} %copy.8.counts_s, s32[1,80]{1,0:T(1,128)} %offsets_h.1, f32[3,1,80]{2,1,0:T(1,128)} %bitcast.65, bf16[1,80,2,4096]{3,2,1,0:T(2,128)(2,1)} %pulses_h.1), custom_call_target="tpu_custom_call" | custom-call | tf_op jit(solution)/shard_map/pallas_call | solution.py:185
  7.5 0.5 %collective-permute-start = (f32[32,512]{1,0:T(8,128)S(1)}, f32[32,512]{1,0:T(8,128)S(1)}, u32[]{:S(2)}, u32[]{:S(2)}) collective-permute-start(f32[32,512]{1,0:T(8,128)S(1)} %get-tuple-element.4), channel_id=1, source_target_pairs={{0,1},{1,0},{2,3},{3,2},{4,5},{5,4},{6,7},{7,6},{8,9},{9,8},{10,11... | collective-permute-start | bytes 196616 | tf_op jit(solution)/shard_map/ppermute | solution.py:212
  8.1 0.9 %collective-permute-done = f32[32,512]{1,0:T(8,128)S(1)} collective-permute-done((f32[32,512]{1,0:T(8,128)S(1)}, f32[32,512]{1,0:T(8,128)S(1)}, u32[]{:S(2)}, u32[]{:S(2)}) %collective-permute-start) | collective-permute-done | bytes 65568 | tf_op jit(solution)/shard_map/ppermute | solution.py:212
  9.0 4.0 %collective-permute-start.2 = (f32[2,32,512]{2,1,0:T(8,128)S(1)}, f32[2,32,512]{2,1,0:T(8,128)S(1)}, u32[]{:S(2)}, u32[]{:S(2)}) collective-permute-start(f32[2,32,512]{2,1,0:T(8,128)S(1)} %pad_maximum_fusion.1), channel_id=1, source_target_pairs={{0,8},{1,9},{2,10},{3,11},{4,12},{5,13},{6,14},{7,15},{8,0},{9,1},... | collective-permute-start | bytes 393224 | tf_op jit(solution)/shard_map/ppermute | solution.py:212
  13.0 1.3 %collective-permute-start.3 = (f32[32,512]{1,0:T(8,128)S(1)}, f32[32,512]{1,0:T(8,128)S(1)}, u32[]{:S(2)}, u32[]{:S(2)}) collective-permute-start(f32[32,512]{1,0:T(8,128)S(1)} %get-tuple-element.12), channel_id=1, source_target_pairs={{0,12},{1,13},{2,14},{3,15},{4,8},{5,9},{6,10},{7,11},{8,4},{9,5},... | collective-permute-start | bytes 196616 | tf_op jit(solution)/shard_map/ppermute | solution.py:212
  14.3 0.2 collective-permute-start.1
  14.6 5.4 %collective-permute-done.3 = f32[32,512]{1,0:T(8,128)S(1)} collective-permute-done((f32[32,512]{1,0:T(8,128)S(1)}, f32[32,512]{1,0:T(8,128)S(1)}, u32[]{:S(2)}, u32[]{:S(2)}) %collective-permute-start.3) | collective-permute-done | bytes 65568 | tf_op jit(solution)/shard_map/ppermute | solution.py:212
  20.0 1.3 %collective-permute-done.1 = f32[32,512]{1,0:T(8,128)S(1)} collective-permute-done((f32[32,512]{1,0:T(8,128)S(1)}, f32[32,512]{1,0:T(8,128)S(1)}, u32[]{:S(2)}, u32[]{:S(2)}) %collective-permute-start.1) | collective-permute-done | bytes 65568 | tf_op jit(solution)/shard_map/ppermute | solution.py:212
  21.2 0.3 %collective-permute-done.2 = f32[2,32,512]{2,1,0:T(8,128)S(1)} collective-permute-done((f32[2,32,512]{2,1,0:T(8,128)S(1)}, f32[2,32,512]{2,1,0:T(8,128)S(1)}, u32[]{:S(2)}, u32[]{:S(2)}) %collective-permute-start.2) | collective-permute-done | bytes 131104 | tf_op jit(solution)/shard_map/ppermute | solution.py:212
  21.6 1.9 %collective-permute-start.4 = (f32[2,32,512]{2,1,0:T(8,128)S(1)}, f32[2,32,512]{2,1,0:T(8,128)S(1)}, u32[]{:S(2)}, u32[]{:S(2)}) collective-permute-start(f32[2,32,512]{2,1,0:T(8,128)S(1)} %pad_maximum_fusion.2), channel_id=1, source_target_pairs={{0,2},{1,3},{2,0},{3,1},{4,6},{5,7},{6,4},{7,5},{8,10},{9,11},{10,... | collective-permute-start | bytes 393224 | tf_op jit(solution)/shard_map/ppermute | solution.py:212
  23.6 3.1 %collective-permute-done.4 = f32[2,32,512]{2,1,0:T(8,128)S(1)} collective-permute-done((f32[2,32,512]{2,1,0:T(8,128)S(1)}, f32[2,32,512]{2,1,0:T(8,128)S(1)}, u32[]{:S(2)}, u32[]{:S(2)}) %collective-permute-start.4) | collective-permute-done | bytes 131104 | tf_op jit(solution)/shard_map/ppermute | solution.py:212
  26.7 0.1 collective-permute-start.5
  26.8 1.3 %collective-permute-done.5 = f32[2,32,512]{2,1,0:T(8,128)S(1)} collective-permute-done((f32[2,32,512]{2,1,0:T(8,128)S(1)}, f32[2,32,512]{2,1,0:T(8,128)S(1)}, u32[]{:S(2)}, u32[]{:S(2)}) %collective-permute-start.5) | collective-permute-done | bytes 131104 | tf_op jit(solution)/shard_map/ppermute | solution.py:212
  28.2 0.7 %fusion.2 = (f32[1,2,32,512]{3,2,1,0:T(8,128)}, f32[1,2,32,512]{3,2,1,0:T(8,128)}) fusion(f32[2,1,32,512]{3,2,0,1:T(8,128)S(1)} %get-tuple-element.14, f32[2,1,32,512]{3,2,0,1:T(8,128)S(1)} %get-tuple-element.15), kind=kLoop, calls=%fused_computation.5 | loop fusion | flops 65536 | bytes 524288
  (7 shorter events, 0.2 us)
Async XLA Ops:
  7.5 1.4 %collective-permute-start = (f32[32,512]{1,0:T(8,128)S(1)}, f32[32,512]{1,0:T(8,128)S(1)}, u32[]{:S(2)}, u32[]{:S(2)}) collective-permute-start(f32[32,512]{1,0:T(8,128)S(1)} %get-tuple-element.4), channel_id=1, source_target_pairs={{0,1},{1,0},{2,3},{3,2},{4,5},{5,4},{6,7},{7,6},{8,9},{9,8},{10,11... | collective-permute-start | bytes 196616 | tf_op jit(solution)/shard_map/ppermute | solution.py:212
  9.0 12.5 %collective-permute-start.2 = (f32[2,32,512]{2,1,0:T(8,128)S(1)}, f32[2,32,512]{2,1,0:T(8,128)S(1)}, u32[]{:S(2)}, u32[]{:S(2)}) collective-permute-start(f32[2,32,512]{2,1,0:T(8,128)S(1)} %pad_maximum_fusion.1), channel_id=1, source_target_pairs={{0,8},{1,9},{2,10},{3,11},{4,12},{5,13},{6,14},{7,15},{8,0},{9,1},... | collective-permute-start | bytes 393224 | tf_op jit(solution)/shard_map/ppermute | solution.py:212
  13.0 7.0 %collective-permute-start.3 = (f32[32,512]{1,0:T(8,128)S(1)}, f32[32,512]{1,0:T(8,128)S(1)}, u32[]{:S(2)}, u32[]{:S(2)}) collective-permute-start(f32[32,512]{1,0:T(8,128)S(1)} %get-tuple-element.12), channel_id=1, source_target_pairs={{0,12},{1,13},{2,14},{3,15},{4,8},{5,9},{6,10},{7,11},{8,4},{9,5},... | collective-permute-start | bytes 196616 | tf_op jit(solution)/shard_map/ppermute | solution.py:212
  14.3 6.9 %collective-permute-start.1 = (f32[32,512]{1,0:T(8,128)S(1)}, f32[32,512]{1,0:T(8,128)S(1)}, u32[]{:S(2)}, u32[]{:S(2)}) collective-permute-start(f32[32,512]{1,0:T(8,128)S(1)} %get-tuple-element.12), channel_id=1, source_target_pairs={{0,4},{1,5},{2,6},{3,7},{4,0},{5,1},{6,2},{7,3},{8,12},{9,13},{10,... | collective-permute-start | bytes 196616 | tf_op jit(solution)/shard_map/ppermute | solution.py:212
  21.6 5.0 %collective-permute-start.4 = (f32[2,32,512]{2,1,0:T(8,128)S(1)}, f32[2,32,512]{2,1,0:T(8,128)S(1)}, u32[]{:S(2)}, u32[]{:S(2)}) collective-permute-start(f32[2,32,512]{2,1,0:T(8,128)S(1)} %pad_maximum_fusion.2), channel_id=1, source_target_pairs={{0,2},{1,3},{2,0},{3,1},{4,6},{5,7},{6,4},{7,5},{8,10},{9,11},{10,... | collective-permute-start | bytes 393224 | tf_op jit(solution)/shard_map/ppermute | solution.py:212
  26.7 1.4 %collective-permute-start.5 = (f32[2,32,512]{2,1,0:T(8,128)S(1)}, f32[2,32,512]{2,1,0:T(8,128)S(1)}, u32[]{:S(2)}, u32[]{:S(2)}) collective-permute-start(f32[2,32,512]{2,1,0:T(8,128)S(1)} %fusion.4), channel_id=1, source_target_pairs={{0,1},{1,0},{2,3},{3,2},{4,5},{5,4},{6,7},{7,6},{8,9},{9,8},{10,11... | collective-permute-start | bytes 393224 | tf_op jit(solution)/shard_map/ppermute | solution.py:212

commit v4 on v3

--- a/solution.py
+++ b/solution.py
@@ -13,7 +13,6 @@
 BINS = 128
 WINDOW = 8
 LANES = 128
-GROUP = 8
 
 SIN = (3.141592580044369, -5.167706878903419, 2.5500313768938527, -0.5980451717629565, 0.07722012423151481)
 COS = (0.999999953468687, -4.934792858755703, 4.0584119149345526, -1.3318801632613946, 0.21969679848706386)
@@ -43,9 +42,11 @@
 
 
 def image_kernel(rows, cols, width, counts_s, offsets_h, geometry_h, pulses_h, kept_ref, sent_ref,
-                 held, window_f32, geometry_v, offsets_v, offsets_s, columns, seeds, steps, acc, sems):
+                 held, window_f32, geometry_v, offsets_v, offsets_s, columns, seeds, steps, sems):
     slots, _, samples = held.shape
     pieces = cols // LANES
+    half_x = rows // 2
+    half_y = LANES // 2
     small = [
         pltpu.make_async_copy(source, target, sems.at[k])
         for k, (source, target) in enumerate((
@@ -81,34 +82,35 @@
     lane = lax.broadcasted_iota(jnp.int32, shape, 1).astype(jnp.float32)
     g = lane - width // 2
     theta = g / width + 0.37
-    y_local = lane
     last_block = samples // LANES - 2
     block = jnp.minimum(jnp.floor(offset / LANES), last_block)
     rest = offset - LANES * block
 
-    angle = slope_c * y_local
-    base = cis_turns(angle * (0.37 - (width // 2) / width))
-    one = cis_turns(angle / width)
-    now = base
-    for r in range(8):
+    def sequence(first_seed, half):
+        one = csquare(half)
+        now = half
+        for r in range(8):
+            for k in range(2):
+                seeds[first_seed + k, pl.ds(r, slots, stride=8), :] = now[k]
+            if r < 7:
+                now = cmul(now, one)
+        return csquare(csquare(csquare(one)))
+
+    def keep(first_step, value):
         for k in range(2):
-            seeds[2 + k, pl.ds(r, slots, stride=8), :] = now[k]
-        if r < 7:
-            now = cmul(now, one)
-    ratio = csquare(csquare(csquare(one)))
-    for level in range(4):
-        for k in range(2):
-            steps[8 + 2 * level + k] = ratio[k]
+            steps[first_step + k] = value[k]
+
+    ratio = sequence(0, cis_turns((0.5 * slope_r) * theta))
+    keep(0, ratio)
+    ratio = sequence(2, cis_turns((0.5 * slope_c) * theta))
+    for level in range(3):
+        keep(2 + 2 * level, ratio)
         ratio = csquare(ratio)
-
-    row_one = cis_turns(theta * slope_r)
-    ratio = csquare(csquare(csquare(row_one)))
-    piece = cis_turns(theta * (slope_c * LANES))
-    for level, value in enumerate((ratio, csquare(ratio), piece, csquare(piece))):
-        for k in range(2):
-            steps[2 * level + k] = value[k]
-
-    phase = theta * ((width / 2.0 + width / 16.0 * geo_centre) - slope_r * (rows // 2) - slope_c * (cols // 2))
+    piece = csquare(ratio)
+
+    phase = theta * (
+        (width / 2.0 + width / 16.0 * geo_centre) - 0.5 * slope_r + slope_c * (half_y - 0.5 - cols // 2)
+    )
     scaled = 37.0 * offset
     steps37 = (scaled - 100.0 * jnp.round(scaled / 100.0)) / 100.0
     circular = g * rest / width
@@ -117,7 +119,7 @@
 
     load.wait()
     for p in range(slots):
-        start = jnp.minimum(offsets_s[0, p] // LANES, last_block) * LANES
+        start = jnp.minimum(offsets_s[0, p] >> 7, last_block) * LANES
         pair = held[p, :, pl.ds(pl.multiple_of(start, LANES), 2 * LANES)].astype(jnp.float32)
         for half in range(2):
             window_f32[half, 2 * p:2 * p + 2, :] = pair[:, half * LANES:(half + 1) * LANES]
@@ -134,47 +136,67 @@
     live = lax.broadcasted_iota(jnp.int32, shape, 0) < counts_s[0]
     scale = jnp.where(live, 1.0 / (width * math.sqrt(slots)), 0.0)
     now = cmul((spectrum[:, 0:LANES] * scale, spectrum[:, LANES:] * scale), phase_cis)
-    for r in range(8):
-        for k in range(2):
-            seeds[k, pl.ds(r, slots, stride=8), :] = now[k]
-        if r < 7:
-            now = cmul(now, row_one)
-
-    acc[...] = jnp.zeros_like(acc)
-
-    def grown(seed, first_step, pulse):
-        values = [seed]
-        for level in range(4):
-            step = tuple(
-                jnp.broadcast_to(steps[first_step + 2 * level + k, pl.ds(pulse, 1), :], (8, LANES)) for k in range(2)
-            )
-            values = values + [cmul(v, step) for v in values]
-        return [jnp.concatenate([v[k] for v in values], axis=0) for k in range(2)]
-
-    def add_group(step, carry):
-        lefts = []
-        rights = []
-        for i in range(GROUP):
-            pulse = step * GROUP + i
-            at = pl.ds(pl.multiple_of(8 * pulse, 8), 8)
-            left = grown((seeds[0, at, :], seeds[1, at, :]), 0, pulse)
-            lefts += [v.astype(jnp.bfloat16) for v in left]
-            right_re, right_im = grown((seeds[2, at, :], seeds[3, at, :]), 8, pulse)
-            rights.append(jnp.concatenate([right_re, right_im], axis=1).astype(jnp.bfloat16))
-            rights.append(jnp.concatenate([-right_im, right_re], axis=1).astype(jnp.bfloat16))
-        acc[...] += jnp.dot(
-            jnp.concatenate(lefts, axis=1), jnp.concatenate(rights, axis=0), preferred_element_type=jnp.float32
-        )
-        return carry
-
-    lax.fori_loop(0, slots // GROUP, add_group, 0)
-    second = lax.rem(lax.axis_index("sub"), 2) == 1
-    for piece_at in range(pieces):
-        at = slice(piece_at * rows, (piece_at + 1) * rows)
-        real, imag = acc[at, 0:LANES], acc[at, LANES:2 * LANES]
-        lanes = slice(piece_at * LANES, (piece_at + 1) * LANES)
-        kept_ref[:, lanes] = jnp.where(second, imag, real)
-        sent_ref[:, lanes] = jnp.where(second, real, imag)
+    for q in range(pieces):
+        keep(8 + 2 * q, now)
+        if q < pieces - 1:
+            now = cmul(now, piece)
+
+    lefts = []
+    rights = []
+    for pulse in range(slots):
+        at = slice(8 * pulse, 8 * pulse + 8)
+
+        def spread(k):
+            return jnp.broadcast_to(steps[k, pulse:pulse + 1, :], (8, LANES))
+
+        values = [(seeds[2, at, :], seeds[3, at, :])]
+        for level in range(3):
+            step_on = (spread(2 + 2 * level), spread(3 + 2 * level))
+            values = values + [cmul(v, step_on) for v in values]
+        rights.append(jnp.concatenate([v[k] for k in range(2) for v in values], axis=0).astype(jnp.bfloat16))
+        values = [(seeds[0, at, :], seeds[1, at, :])]
+        step_on = (spread(0), spread(1))
+        while len(values) * 8 < half_x:
+            values.append(cmul(values[-1], step_on))
+        products = []
+        for q in range(pieces):
+            for t in range(2):
+                factor = spread(8 + 2 * q + t)
+                products += [factor * v[k] for k in range(2) for v in values]
+        lefts.append(jnp.concatenate(products, axis=0).astype(jnp.bfloat16))
+    acc = lax.dot_general(
+        jnp.concatenate(lefts, axis=1), jnp.concatenate(rights, axis=1), (((1,), (1,)), ((), ())),
+        preferred_element_type=jnp.float32,
+    )
+
+    lanes = lax.broadcasted_iota(jnp.int32, (8, LANES), 1)
+    backward = LANES - 1 - lanes
+    rolled_backward = lax.rem(backward + half_y, LANES)
+    upside_down = 7 - lax.broadcasted_iota(jnp.int32, (8, LANES), 0)
+    in_low = lanes < half_y
+    is_second = lax.rem(lax.axis_index("sub"), 2) == 1
+    for q in range(pieces):
+        base = q * 4 * half_x
+        for r in range(half_x // 8):
+            ac, as_, bc, bs = (acc[base + n * half_x + 8 * r:base + n * half_x + 8 * r + 8, :] for n in range(4))
+            for side in range(2):
+                sign = 1.0 if side else -1.0
+                both = []
+                for real in range(2):
+                    if real:
+                        v = jnp.where(in_low, ac - sign * bs, -sign * as_ - bc)
+                    else:
+                        v = jnp.where(in_low, bc + sign * as_, ac - sign * bs)
+                    ahead = v + pltpu.roll(v, half_y, 1)
+                    behind = jnp.take_along_axis(v, rolled_backward, axis=1) - jnp.take_along_axis(v, backward, axis=1)
+                    both.append(jnp.where(in_low, behind, ahead))
+                if not side:
+                    both = [jnp.take_along_axis(v, upside_down, axis=0) for v in both]
+                imag, real = both
+                row = half_x + 8 * r if side else half_x - 8 * (r + 1)
+                at = (slice(row, row + 8), slice(q * LANES, (q + 1) * LANES))
+                kept_ref[at] = jnp.where(is_second, imag, real)
+                sent_ref[at] = jnp.where(is_second, real, imag)
 
 
 def halves_of_image(pulses, offsets, geometry, counts):
@@ -196,7 +218,6 @@
             pltpu.VMEM((LANES, LANES), jnp.float32),
             pltpu.VMEM((4, 8 * slots, LANES), jnp.float32),
             pltpu.VMEM((16, slots, LANES), jnp.float32),
-            pltpu.VMEM((COLS // LANES * ROWS, 2 * LANES), jnp.float32),
             pltpu.SemaphoreType.DMA((4,)),
         ],
         compiler_params=pltpu.CompilerParams(vmem_limit_bytes=40 * 1024 * 1024),

time: 29.4 us -> 26.6 us (0.905)
  Pallas kernels: 6.25 us -> 3.47 us
    pallas_call x1, Pallas kernels: 6.25 us -> 3.47 us  [halves_of_image(): pl.pallas_call(functools.partial(image_kernel, ROWS, COLS, BINS), out_sha...]
where the time goes in v4:
time: 26.6 us; the launch traced here: 26.1 us
  waiting for transfers between devices  12.3 us (46%)
  starting transfers between devices  8.04 us (30%)
  Pallas kernels  3.47 us (13%)
  between operations  1.43 us (5%)
  other arithmetic  0.88 us (3%)
    ppermute x6, waiting for transfers between devices, swap(): lax.ppermute(value, 'sub', [(i, i ^ distance) for i in range(members)])  12.3 us
    ppermute x6, starting transfers between devices, swap(): lax.ppermute(value, 'sub', [(i, i ^ distance) for i in range(members)])  8.04 us
    pallas_call x1, Pallas kernels, halves_of_image(): pl.pallas_call(functools.partial(image_kernel, ROWS, COLS, BINS), out_sha...  3.47 us
    unnamed x1, other arithmetic  0.72 us
  transfers between devices with their start and end apart: 6, of which 6 were waited for; matrix products, arithmetic and copies ran while one was open for 0% of the time, Pallas kernels for 0%

profile of v4, /device:TPU:0, one launch (start us, length us, event | category | flops | bytes accessed | tf_op | source)
XLA Modules:
  0.0 26.1 jit_solution(2498634792418564903)
XLA Ops:
  1.3 3.5 %shard_map.59 = (f32[32,512]{1,0:T(8,128)S(1)}, f32[32,512]{1,0:T(8,128)S(1)}) custom-call(s32[1]{0:T(128)S(6)} %copy.8.counts_s, s32[1,80]{1,0:T(1,128)} %offsets_h.1, f32[3,1,80]{2,1,0:T(1,128)} %bitcast.65, bf16[1,80,2,4096]{3,2,1,0:T(2,128)(2,1)} %pulses_h.1), custom_call_target="tpu_custom_call" | custom-call | tf_op jit(solution)/shard_map/pallas_call | solution.py:207
  4.8 0.5 %collective-permute-start = (f32[32,512]{1,0:T(8,128)S(1)}, f32[32,512]{1,0:T(8,128)S(1)}, u32[]{:S(2)}, u32[]{:S(2)}) collective-permute-start(f32[32,512]{1,0:T(8,128)S(1)} %get-tuple-element.4), channel_id=1, source_target_pairs={{0,1},{1,0},{2,3},{3,2},{4,5},{5,4},{6,7},{7,6},{8,9},{9,8},{10,11... | collective-permute-start | bytes 196616 | tf_op jit(solution)/shard_map/ppermute | solution.py:233
  5.3 0.9 %collective-permute-done = f32[32,512]{1,0:T(8,128)S(1)} collective-permute-done((f32[32,512]{1,0:T(8,128)S(1)}, f32[32,512]{1,0:T(8,128)S(1)}, u32[]{:S(2)}, u32[]{:S(2)}) %collective-permute-start) | collective-permute-done | bytes 65568 | tf_op jit(solution)/shard_map/ppermute | solution.py:233
  6.2 4.0 %collective-permute-start.2 = (f32[2,32,512]{2,1,0:T(8,128)S(1)}, f32[2,32,512]{2,1,0:T(8,128)S(1)}, u32[]{:S(2)}, u32[]{:S(2)}) collective-permute-start(f32[2,32,512]{2,1,0:T(8,128)S(1)} %pad_maximum_fusion.1), channel_id=1, source_target_pairs={{0,8},{1,9},{2,10},{3,11},{4,12},{5,13},{6,14},{7,15},{8,0},{9,1},... | collective-permute-start | bytes 393224 | tf_op jit(solution)/shard_map/ppermute | solution.py:233
  10.2 1.3 %collective-permute-start.3 = (f32[32,512]{1,0:T(8,128)S(1)}, f32[32,512]{1,0:T(8,128)S(1)}, u32[]{:S(2)}, u32[]{:S(2)}) collective-permute-start(f32[32,512]{1,0:T(8,128)S(1)} %get-tuple-element.12), channel_id=1, source_target_pairs={{0,12},{1,13},{2,14},{3,15},{4,8},{5,9},{6,10},{7,11},{8,4},{9,5},... | collective-permute-start | bytes 196616 | tf_op jit(solution)/shard_map/ppermute | solution.py:233
  11.6 0.2 collective-permute-start.1
  11.8 5.4 %collective-permute-done.3 = f32[32,512]{1,0:T(8,128)S(1)} collective-permute-done((f32[32,512]{1,0:T(8,128)S(1)}, f32[32,512]{1,0:T(8,128)S(1)}, u32[]{:S(2)}, u32[]{:S(2)}) %collective-permute-start.3) | collective-permute-done | bytes 65568 | tf_op jit(solution)/shard_map/ppermute | solution.py:233
  17.2 1.3 %collective-permute-done.1 = f32[32,512]{1,0:T(8,128)S(1)} collective-permute-done((f32[32,512]{1,0:T(8,128)S(1)}, f32[32,512]{1,0:T(8,128)S(1)}, u32[]{:S(2)}, u32[]{:S(2)}) %collective-permute-start.1) | collective-permute-done | bytes 65568 | tf_op jit(solution)/shard_map/ppermute | solution.py:233
  18.5 0.3 %collective-permute-done.2 = f32[2,32,512]{2,1,0:T(8,128)S(1)} collective-permute-done((f32[2,32,512]{2,1,0:T(8,128)S(1)}, f32[2,32,512]{2,1,0:T(8,128)S(1)}, u32[]{:S(2)}, u32[]{:S(2)}) %collective-permute-start.2) | collective-permute-done | bytes 131104 | tf_op jit(solution)/shard_map/ppermute | solution.py:233
  18.8 1.9 %collective-permute-start.4 = (f32[2,32,512]{2,1,0:T(8,128)S(1)}, f32[2,32,512]{2,1,0:T(8,128)S(1)}, u32[]{:S(2)}, u32[]{:S(2)}) collective-permute-start(f32[2,32,512]{2,1,0:T(8,128)S(1)} %pad_maximum_fusion.2), channel_id=1, source_target_pairs={{0,2},{1,3},{2,0},{3,1},{4,6},{5,7},{6,4},{7,5},{8,10},{9,11},{10,... | collective-permute-start | bytes 393224 | tf_op jit(solution)/shard_map/ppermute | solution.py:233
  20.8 3.1 %collective-permute-done.4 = f32[2,32,512]{2,1,0:T(8,128)S(1)} collective-permute-done((f32[2,32,512]{2,1,0:T(8,128)S(1)}, f32[2,32,512]{2,1,0:T(8,128)S(1)}, u32[]{:S(2)}, u32[]{:S(2)}) %collective-permute-start.4) | collective-permute-done | bytes 131104 | tf_op jit(solution)/shard_map/ppermute | solution.py:233
  23.9 0.1 collective-permute-start.5
  24.0 1.3 %collective-permute-done.5 = f32[2,32,512]{2,1,0:T(8,128)S(1)} collective-permute-done((f32[2,32,512]{2,1,0:T(8,128)S(1)}, f32[2,32,512]{2,1,0:T(8,128)S(1)}, u32[]{:S(2)}, u32[]{:S(2)}) %collective-permute-start.5) | collective-permute-done | bytes 131104 | tf_op jit(solution)/shard_map/ppermute | solution.py:233
  25.4 0.7 %fusion.2 = (f32[1,2,32,512]{3,2,1,0:T(8,128)}, f32[1,2,32,512]{3,2,1,0:T(8,128)}) fusion(f32[2,1,32,512]{3,2,0,1:T(8,128)S(1)} %get-tuple-element.14, f32[2,1,32,512]{3,2,0,1:T(8,128)S(1)} %get-tuple-element.15), kind=kLoop, calls=%fused_computation.5 | loop fusion | flops 65536 | bytes 524288
  (7 shorter events, 0.2 us)
Async XLA Ops:
  4.8 1.4 %collective-permute-start = (f32[32,512]{1,0:T(8,128)S(1)}, f32[32,512]{1,0:T(8,128)S(1)}, u32[]{:S(2)}, u32[]{:S(2)}) collective-permute-start(f32[32,512]{1,0:T(8,128)S(1)} %get-tuple-element.4), channel_id=1, source_target_pairs={{0,1},{1,0},{2,3},{3,2},{4,5},{5,4},{6,7},{7,6},{8,9},{9,8},{10,11... | collective-permute-start | bytes 196616 | tf_op jit(solution)/shard_map/ppermute | solution.py:233
  6.2 12.5 %collective-permute-start.2 = (f32[2,32,512]{2,1,0:T(8,128)S(1)}, f32[2,32,512]{2,1,0:T(8,128)S(1)}, u32[]{:S(2)}, u32[]{:S(2)}) collective-permute-start(f32[2,32,512]{2,1,0:T(8,128)S(1)} %pad_maximum_fusion.1), channel_id=1, source_target_pairs={{0,8},{1,9},{2,10},{3,11},{4,12},{5,13},{6,14},{7,15},{8,0},{9,1},... | collective-permute-start | bytes 393224 | tf_op jit(solution)/shard_map/ppermute | solution.py:233
  10.2 7.0 %collective-permute-start.3 = (f32[32,512]{1,0:T(8,128)S(1)}, f32[32,512]{1,0:T(8,128)S(1)}, u32[]{:S(2)}, u32[]{:S(2)}) collective-permute-start(f32[32,512]{1,0:T(8,128)S(1)} %get-tuple-element.12), channel_id=1, source_target_pairs={{0,12},{1,13},{2,14},{3,15},{4,8},{5,9},{6,10},{7,11},{8,4},{9,5},... | collective-permute-start | bytes 196616 | tf_op jit(solution)/shard_map/ppermute | solution.py:233
  11.6 6.9 %collective-permute-start.1 = (f32[32,512]{1,0:T(8,128)S(1)}, f32[32,512]{1,0:T(8,128)S(1)}, u32[]{:S(2)}, u32[]{:S(2)}) collective-permute-start(f32[32,512]{1,0:T(8,128)S(1)} %get-tuple-element.12), channel_id=1, source_target_pairs={{0,4},{1,5},{2,6},{3,7},{4,0},{5,1},{6,2},{7,3},{8,12},{9,13},{10,... | collective-permute-start | bytes 196616 | tf_op jit(solution)/shard_map/ppermute | solution.py:233
  18.8 5.0 %collective-permute-start.4 = (f32[2,32,512]{2,1,0:T(8,128)S(1)}, f32[2,32,512]{2,1,0:T(8,128)S(1)}, u32[]{:S(2)}, u32[]{:S(2)}) collective-permute-start(f32[2,32,512]{2,1,0:T(8,128)S(1)} %pad_maximum_fusion.2), channel_id=1, source_target_pairs={{0,2},{1,3},{2,0},{3,1},{4,6},{5,7},{6,4},{7,5},{8,10},{9,11},{10,... | collective-permute-start | bytes 393224 | tf_op jit(solution)/shard_map/ppermute | solution.py:233
  23.9 1.4 %collective-permute-start.5 = (f32[2,32,512]{2,1,0:T(8,128)S(1)}, f32[2,32,512]{2,1,0:T(8,128)S(1)}, u32[]{:S(2)}, u32[]{:S(2)}) collective-permute-start(f32[2,32,512]{2,1,0:T(8,128)S(1)} %fusion.4), channel_id=1, source_target_pairs={{0,1},{1,0},{2,3},{3,2},{4,5},{5,4},{6,7},{7,6},{8,9},{9,8},{10,11... | collective-permute-start | bytes 393224 | tf_op jit(solution)/shard_map/ppermute | solution.py:233

commit v5 on v4

--- a/solution.py
+++ b/solution.py
@@ -239,6 +239,10 @@
     upper = me // 2 % 2 == 1
     block = me // 4
     blocks = members // 4
+    reach = WINDOW - 1
+    links = [(i, i + reach) for i in range(1, members - reach, 2)]
+    whole = jnp.where(odd, jnp.stack([sent, kept]), 0.0)
+    oldest = lax.ppermute(whole, "sub", links)
     got = swap(sent, 1)
     first = jnp.where(odd, got, kept)
     second = jnp.where(odd, kept, got)
@@ -246,20 +250,18 @@
 
     if blocks <= 4:
         nothing = jnp.zeros_like(pair)
-        earlier = last = before_last = oldest = nothing
-        for k in range(1, blocks):
-            value = jnp.stack([pair, second]) if k == 2 else pair
-            value = swap(value, 4 * k)
+        earlier = last = before_last = nothing
+        for k in range(blocks - 1, 0, -1):
             if k == 2:
-                oldest = jnp.where(block >= 2, value[1], nothing)
-                value = value[0]
-                before_last = jnp.where(block >= 2, value, nothing)
+                value = before_last = ahead(pair, 8)
+            else:
+                value = swap(pair, 4 * k)
             source = block ^ k
             earlier = earlier + jnp.where(source < block, value, nothing)
             last = last + jnp.where(source == block - 1, value, nothing)
     else:
         last = ahead(pair, 4)
-        before_last, oldest = ahead(jnp.stack([pair, second]), 8)
+        before_last = ahead(pair, 8)
         earlier = last
         distance = 4
         while distance < members:
@@ -271,18 +273,20 @@
         last + jnp.where(upper, before_last, pair),
     ])
     other = swap(mine, 2)
+    other, oldest = lax.optimization_barrier((other, oldest))
     earlier = earlier + other[0]
     recent = last + other[1]
     frame_scale = 1.0 / math.sqrt(WINDOW)
     number = (me - me % 2 + 1).astype(jnp.float32)
-    firsts = jnp.stack([(first + recent + oldest) * frame_scale, (earlier + first) / jnp.sqrt(number)])
+    firsts = jnp.stack([(first + recent) * frame_scale, (earlier + first) / jnp.sqrt(number)])
     seconds = jnp.stack([(pair + recent) * frame_scale, (earlier + pair) / jnp.sqrt(number + 1.0)])
 
     own = jnp.where(odd, seconds, firsts)
     back = swap(jnp.where(odd, firsts, seconds), 1)
     real = jnp.where(odd, back, own)
     imag = jnp.where(odd, own, back)
-    frames, cumulative = jnp.stack([real, imag], axis=1)
+    frames = jnp.stack([real[0] + oldest[0] * frame_scale, imag[0] + oldest[1] * frame_scale])
+    cumulative = jnp.stack([real[1], imag[1]])
     return frames[None], cumulative[None]
 
 

time: 26.6 us -> 24.4 us (0.917); the launches traced: 26.1 us -> 24.2 us
  waiting for transfers between devices: 12.3 us -> 7.95 us
  starting transfers between devices: 8.04 us -> 10.4 us
    ppermute x6 -> x5, waiting for transfers between devices: 12.3 us -> 7.48 us  [swap(): lax.ppermute(value, 'sub', [(i, i ^ distance) for i in range(members)])]
    ppermute x0 -> x2, starting transfers between devices: none -> 2 us  [the longest x1 1.33 us: ahead(): lax.ppermute(value, 'sub', [(i, i + distance) for i in range(members - di...]
    broadcast_in_dim x0 -> x1, other arithmetic: none -> 0.72 us  [shards(): return (frames[None], cumulative[None])]
    unnamed x1 -> x0, other arithmetic: 0.72 us -> none
    ppermute x0 -> x2, waiting for transfers between devices: none -> 0.47 us  [the longest x1 0.47 us: ahead(): lax.ppermute(value, 'sub', [(i, i + distance) for i in range(members - di...]
    ppermute x6 -> x5, starting transfers between devices: 8.04 us -> 8.41 us  [swap(): lax.ppermute(value, 'sub', [(i, i ^ distance) for i in range(members)])]
  transfers between devices with their start and end apart: 6 -> 7, of which waited for: 6 -> 5; matrix products, arithmetic and copies ran while one was open for 0% -> 0% of each run, Pallas kernels for 0% -> 0%
where the time goes in v5:
time: 24.4 us; the launch traced here: 24.2 us
  starting transfers between devices  10.4 us (43%)
  waiting for transfers between devices  7.95 us (33%)
  Pallas kernels  3.47 us (14%)
  between operations  1.5 us (6%)
  other arithmetic  0.91 us (4%)
    ppermute x5, starting transfers between devices, swap(): lax.ppermute(value, 'sub', [(i, i ^ distance) for i in range(members)])  8.41 us
    ppermute x5, waiting for transfers between devices, swap(): lax.ppermute(value, 'sub', [(i, i ^ distance) for i in range(members)])  7.48 us
    pallas_call x1, Pallas kernels, halves_of_image(): pl.pallas_call(functools.partial(image_kernel, ROWS, COLS, BINS), out_sha...  3.47 us
    ppermute x1, starting transfers between devices, ahead(): lax.ppermute(value, 'sub', [(i, i + distance) for i in range(members - di...  1.33 us
    broadcast_in_dim x1, other arithmetic, shards(): return (frames[None], cumulative[None])  0.72 us
    ppermute x1, starting transfers between devices, shards(): oldest = lax.ppermute(whole, 'sub', links)  0.67 us
  transfers between devices with their start and end apart: 7, of which 5 were waited for; matrix products, arithmetic and copies ran while one was open for 0% of the time, Pallas kernels for 0%

profile of v5, /device:TPU:0, one launch (start us, length us, event | category | flops | bytes accessed | tf_op | source)
XLA Modules:
  0.0 24.2 jit_solution(6546611368067670186)
XLA Ops:
  1.3 3.5 %shard_map.59 = (f32[32,512]{1,0:T(8,128)S(1)}, f32[32,512]{1,0:T(8,128)S(1)}) custom-call(s32[1]{0:T(128)S(6)} %copy.6.counts_s, s32[1,80]{1,0:T(1,128)} %offsets_h.1, f32[3,1,80]{2,1,0:T(1,128)} %bitcast.33, bf16[1,80,2,4096]{3,2,1,0:T(2,128)(2,1)} %pulses_h.1), custom_call_target="tpu_custom_call" | custom-call | tf_op jit(solution)/shard_map/pallas_call | solution.py:207
  4.8 0.5 %collective-permute-start = (f32[32,512]{1,0:T(8,128)S(1)}, f32[32,512]{1,0:T(8,128)S(1)}, u32[]{:S(2)}, u32[]{:S(2)}) collective-permute-start(f32[32,512]{1,0:T(8,128)S(1)} %get-tuple-element.6), channel_id=1, source_target_pairs={{0,1},{1,0},{2,3},{3,2},{4,5},{5,4},{6,7},{7,6},{8,9},{9,8},{10,11... | collective-permute-start | bytes 196616 | tf_op jit(solution)/shard_map/ppermute | solution.py:233
  5.3 0.9 %collective-permute-done = f32[32,512]{1,0:T(8,128)S(1)} collective-permute-done((f32[32,512]{1,0:T(8,128)S(1)}, f32[32,512]{1,0:T(8,128)S(1)}, u32[]{:S(2)}, u32[]{:S(2)}) %collective-permute-start) | collective-permute-done | bytes 65568 | tf_op jit(solution)/shard_map/ppermute | solution.py:233
  6.2 5.0 %collective-permute-start.1 = (f32[32,512]{1,0:T(8,128)S(1)}, f32[32,512]{1,0:T(8,128)S(1)}, u32[]{:S(2)}, u32[]{:S(2)}) collective-permute-start(f32[32,512]{1,0:T(8,128)S(1)} %select_add_fusion.2), channel_id=1, source_target_pairs={{0,12},{1,13},{2,14},{3,15},{4,8},{5,9},{6,10},{7,11},{8,4},{9,5},... | collective-permute-start | bytes 196616 | tf_op jit(solution)/shard_map/ppermute | solution.py:233
  11.2 1.3 %collective-permute-start.2 = (f32[32,512]{1,0:T(8,128)S(1)}, f32[32,512]{1,0:T(8,128)S(1)}, u32[]{:S(2)}, u32[]{:S(2)}) collective-permute-start(f32[32,512]{1,0:T(8,128)S(1)} %select_add_fusion.2), channel_id=1, source_target_pairs={{0,8},{1,9},{2,10},{3,11},{4,12},{5,13},{6,14},{7,15},{16,24},{17,... | collective-permute-start | bytes 196616 | tf_op jit(solution)/shard_map/ppermute | solution.py:236
  12.5 1.2 %collective-permute-start.3 = (f32[32,512]{1,0:T(8,128)S(1)}, f32[32,512]{1,0:T(8,128)S(1)}, u32[]{:S(2)}, u32[]{:S(2)}) collective-permute-start(f32[32,512]{1,0:T(8,128)S(1)} %select_add_fusion.2), channel_id=1, source_target_pairs={{0,4},{1,5},{2,6},{3,7},{4,0},{5,1},{6,2},{7,3},{8,12},{9,13},{10,... | collective-permute-start | bytes 196616 | tf_op jit(solution)/shard_map/ppermute | solution.py:233
  13.8 0.7 %collective-permute-start.5 = (f32[2,32,512]{2,1,0:T(8,128)S(1)}, f32[2,32,512]{2,1,0:T(8,128)S(1)}, u32[]{:S(2)}, u32[]{:S(2)}) collective-permute-start(f32[2,32,512]{2,1,0:T(8,128)S(1)} %maximum_select_fusion), channel_id=1, source_target_pairs={{1,8},{3,10},{5,12},{7,14},{17,24},{19,26},{21,28},{23,30}} | collective-permute-start | bytes 393224 | tf_op jit(solution)/shard_map/ppermute | solution.py:245
  14.5 0.0 collective-permute-done.1
  14.5 0.5 %collective-permute-done.2 = f32[32,512]{1,0:T(8,128)S(1)} collective-permute-done((f32[32,512]{1,0:T(8,128)S(1)}, f32[32,512]{1,0:T(8,128)S(1)}, u32[]{:S(2)}, u32[]{:S(2)}) %collective-permute-start.2) | collective-permute-done | bytes 65568 | tf_op jit(solution)/shard_map/ppermute | solution.py:236
  15.0 1.9 %collective-permute-done.3 = f32[32,512]{1,0:T(8,128)S(1)} collective-permute-done((f32[32,512]{1,0:T(8,128)S(1)}, f32[32,512]{1,0:T(8,128)S(1)}, u32[]{:S(2)}, u32[]{:S(2)}) %collective-permute-start.3) | collective-permute-done | bytes 65568 | tf_op jit(solution)/shard_map/ppermute | solution.py:233
  16.9 1.6 %collective-permute-start.4 = (f32[2,32,512]{2,1,0:T(8,128)S(1)}, f32[2,32,512]{2,1,0:T(8,128)S(1)}, u32[]{:S(2)}, u32[]{:S(2)}) collective-permute-start(f32[2,32,512]{2,1,0:T(8,128)S(1)} %pad_maximum_fusion), channel_id=1, source_target_pairs={{0,2},{1,3},{2,0},{3,1},{4,6},{5,7},{6,4},{7,5},{8,10},{9,11},{10,... | collective-permute-start | bytes 393224 | tf_op jit(solution)/shard_map/ppermute | solution.py:233
  18.6 0.0 collective-permute-done.5
  18.6 3.3 %collective-permute-done.4 = f32[2,32,512]{2,1,0:T(8,128)S(1)} collective-permute-done((f32[2,32,512]{2,1,0:T(8,128)S(1)}, f32[2,32,512]{2,1,0:T(8,128)S(1)}, u32[]{:S(2)}, u32[]{:S(2)}) %collective-permute-start.4) | collective-permute-done | bytes 131104 | tf_op jit(solution)/shard_map/ppermute | solution.py:233
  22.0 0.1 collective-permute-start.6
  22.1 1.3 %collective-permute-done.6 = f32[2,32,512]{2,1,0:T(8,128)S(1)} collective-permute-done((f32[2,32,512]{2,1,0:T(8,128)S(1)}, f32[2,32,512]{2,1,0:T(8,128)S(1)}, u32[]{:S(2)}, u32[]{:S(2)}) %collective-permute-start.6) | collective-permute-done | bytes 131104 | tf_op jit(solution)/shard_map/ppermute | solution.py:233
  23.5 0.7 %maximum_bitcast_fusion = (f32[1,2,32,512]{3,2,1,0:T(8,128)}, f32[1,2,32,512]{3,2,1,0:T(8,128)}) fusion(f32[1,32,512]{2,1,0:T(8,128)S(1)} %get-tuple-element.24, f32[1,32,512]{2,1,0:T(8,128)S(1)} %get-tuple-element.23, f32[1,32,512]{2,1,0:T(8,128)S(1)} %get-tuple-element.25, f32[1,32,512]{2,1,0:T(8,128)S(1)} %get-tuple-element.22), kind=kLoop, calls=%fused_computation.4 | loop fusion | flops 65536 | bytes 524288 | tf_op jit(solution)/shard_map/broadcast_in_dim | solution.py:290
  (8 shorter events, 0.2 us)
Async XLA Ops:
  4.8 1.4 %collective-permute-start = (f32[32,512]{1,0:T(8,128)S(1)}, f32[32,512]{1,0:T(8,128)S(1)}, u32[]{:S(2)}, u32[]{:S(2)}) collective-permute-start(f32[32,512]{1,0:T(8,128)S(1)} %get-tuple-element.6), channel_id=1, source_target_pairs={{0,1},{1,0},{2,3},{3,2},{4,5},{5,4},{6,7},{7,6},{8,9},{9,8},{10,11... | collective-permute-start | bytes 196616 | tf_op jit(solution)/shard_map/ppermute | solution.py:233
  6.2 8.3 %collective-permute-start.1 = (f32[32,512]{1,0:T(8,128)S(1)}, f32[32,512]{1,0:T(8,128)S(1)}, u32[]{:S(2)}, u32[]{:S(2)}) collective-permute-start(f32[32,512]{1,0:T(8,128)S(1)} %select_add_fusion.2), channel_id=1, source_target_pairs={{0,12},{1,13},{2,14},{3,15},{4,8},{5,9},{6,10},{7,11},{8,4},{9,5},... | collective-permute-start | bytes 196616 | tf_op jit(solution)/shard_map/ppermute | solution.py:233
  11.2 3.8 %collective-permute-start.2 = (f32[32,512]{1,0:T(8,128)S(1)}, f32[32,512]{1,0:T(8,128)S(1)}, u32[]{:S(2)}, u32[]{:S(2)}) collective-permute-start(f32[32,512]{1,0:T(8,128)S(1)} %select_add_fusion.2), channel_id=1, source_target_pairs={{0,8},{1,9},{2,10},{3,11},{4,12},{5,13},{6,14},{7,15},{16,24},{17,... | collective-permute-start | bytes 196616 | tf_op jit(solution)/shard_map/ppermute | solution.py:236
  12.5 4.3 %collective-permute-start.3 = (f32[32,512]{1,0:T(8,128)S(1)}, f32[32,512]{1,0:T(8,128)S(1)}, u32[]{:S(2)}, u32[]{:S(2)}) collective-permute-start(f32[32,512]{1,0:T(8,128)S(1)} %select_add_fusion.2), channel_id=1, source_target_pairs={{0,4},{1,5},{2,6},{3,7},{4,0},{5,1},{6,2},{7,3},{8,12},{9,13},{10,... | collective-permute-start | bytes 196616 | tf_op jit(solution)/shard_map/ppermute | solution.py:233
  13.8 4.8 %collective-permute-start.5 = (f32[2,32,512]{2,1,0:T(8,128)S(1)}, f32[2,32,512]{2,1,0:T(8,128)S(1)}, u32[]{:S(2)}, u32[]{:S(2)}) collective-permute-start(f32[2,32,512]{2,1,0:T(8,128)S(1)} %maximum_select_fusion), channel_id=1, source_target_pairs={{1,8},{3,10},{5,12},{7,14},{17,24},{19,26},{21,28},{23,30}} | collective-permute-start | bytes 393224 | tf_op jit(solution)/shard_map/ppermute | solution.py:245
  16.9 5.0 %collective-permute-start.4 = (f32[2,32,512]{2,1,0:T(8,128)S(1)}, f32[2,32,512]{2,1,0:T(8,128)S(1)}, u32[]{:S(2)}, u32[]{:S(2)}) collective-permute-start(f32[2,32,512]{2,1,0:T(8,128)S(1)} %pad_maximum_fusion), channel_id=1, source_target_pairs={{0,2},{1,3},{2,0},{3,1},{4,6},{5,7},{6,4},{7,5},{8,10},{9,11},{10,... | collective-permute-start | bytes 393224 | tf_op jit(solution)/shard_map/ppermute | solution.py:233
  22.0 1.4 %collective-permute-start.6 = (f32[2,32,512]{2,1,0:T(8,128)S(1)}, f32[2,32,512]{2,1,0:T(8,128)S(1)}, u32[]{:S(2)}, u32[]{:S(2)}) collective-permute-start(f32[2,32,512]{2,1,0:T(8,128)S(1)} %fusion.1), channel_id=1, source_target_pairs={{0,1},{1,0},{2,3},{3,2},{4,5},{5,4},{6,7},{7,6},{8,9},{9,8},{10,11... | collective-permute-start | bytes 393224 | tf_op jit(solution)/shard_map/ppermute | solution.py:233

commit v6 on v5

--- a/solution.py
+++ b/solution.py
@@ -58,17 +58,8 @@
     load = pltpu.make_async_copy(pulses_h.at[0], held, sems.at[3])
     load.start()
 
-    b_index = lax.broadcasted_iota(jnp.int32, (width, width), 0).astype(jnp.float32)
-    g_index = lax.broadcasted_iota(jnp.int32, (width, width), 1).astype(jnp.float32) - width // 2
-    cosine, sine = cis_turns(b_index * g_index / width)
-    fourier = jnp.concatenate(
-        [jnp.concatenate([cosine, -sine], axis=1), jnp.concatenate([sine, cosine], axis=1)], axis=0
-    )
-    fourier_high = fourier.astype(jnp.bfloat16)
-    fourier_low = (fourier - fourier_high.astype(jnp.float32)).astype(jnp.bfloat16)
-
     columns[...] = jnp.zeros_like(columns)
-    for copy in small:
+    for copy in small[:2]:
         copy.wait()
     for k in range(3):
         columns[k:k + 1, 0:slots] = geometry_v[k]
@@ -117,6 +108,16 @@
     phase = phase + (circular - jnp.round(circular)) + steps37
     phase_cis = cis_turns(phase)
 
+    b_index = lax.broadcasted_iota(jnp.int32, (width, width), 0).astype(jnp.float32)
+    g_index = lax.broadcasted_iota(jnp.int32, (width, width), 1).astype(jnp.float32) - width // 2
+    cosine, sine = cis_turns(b_index * g_index / width)
+    fourier = jnp.concatenate(
+        [jnp.concatenate([cosine, -sine], axis=1), jnp.concatenate([sine, cosine], axis=1)], axis=0
+    )
+    fourier_high = fourier.astype(jnp.bfloat16)
+    fourier_low = (fourier - fourier_high.astype(jnp.float32)).astype(jnp.bfloat16)
+
+    small[2].wait()
     load.wait()
     for p in range(slots):
         start = jnp.minimum(offsets_s[0, p] >> 7, last_block) * LANES

time: 24.4 us -> 24.4 us (level)
  no operation moved by 1% of the time
where the time goes in v6:
time: 24.4 us; the launch traced here: 24.2 us
  starting transfers between devices  10.4 us (43%)
  waiting for transfers between devices  7.95 us (33%)
  Pallas kernels  3.48 us (14%)
  between operations  1.5 us (6%)
  other arithmetic  0.91 us (4%)
    ppermute x5, starting transfers between devices, swap(): lax.ppermute(value, 'sub', [(i, i ^ distance) for i in range(members)])  8.41 us
    ppermute x5, waiting for transfers between devices, swap(): lax.ppermute(value, 'sub', [(i, i ^ distance) for i in range(members)])  7.48 us
    pallas_call x1, Pallas kernels, halves_of_image(): pl.pallas_call(functools.partial(image_kernel, ROWS, COLS, BINS), out_sha...  3.48 us
    ppermute x1, starting transfers between devices, ahead(): lax.ppermute(value, 'sub', [(i, i + distance) for i in range(members - di...  1.33 us
    broadcast_in_dim x1, other arithmetic, shards(): return (frames[None], cumulative[None])  0.72 us
    ppermute x1, starting transfers between devices, shards(): oldest = lax.ppermute(whole, 'sub', links)  0.67 us
  transfers between devices with their start and end apart: 7, of which 5 were waited for; matrix products, arithmetic and copies ran while one was open for 0% of the time, Pallas kernels for 0%

profile of v6, /device:TPU:0, one launch (start us, length us, event | category | flops | bytes accessed | tf_op | source)
XLA Modules:
  0.0 24.2 jit_solution(6878652421692518016)
XLA Ops:
  1.3 3.5 %shard_map.59 = (f32[32,512]{1,0:T(8,128)S(1)}, f32[32,512]{1,0:T(8,128)S(1)}) custom-call(s32[1]{0:T(128)S(6)} %copy.6.counts_s, s32[1,80]{1,0:T(1,128)} %offsets_h.1, f32[3,1,80]{2,1,0:T(1,128)} %bitcast.33, bf16[1,80,2,4096]{3,2,1,0:T(2,128)(2,1)} %pulses_h.1), custom_call_target="tpu_custom_call" | custom-call | tf_op jit(solution)/shard_map/pallas_call | solution.py:208
  4.8 0.5 %collective-permute-start = (f32[32,512]{1,0:T(8,128)S(1)}, f32[32,512]{1,0:T(8,128)S(1)}, u32[]{:S(2)}, u32[]{:S(2)}) collective-permute-start(f32[32,512]{1,0:T(8,128)S(1)} %get-tuple-element.6), channel_id=1, source_target_pairs={{0,1},{1,0},{2,3},{3,2},{4,5},{5,4},{6,7},{7,6},{8,9},{9,8},{10,11... | collective-permute-start | bytes 196616 | tf_op jit(solution)/shard_map/ppermute | solution.py:234
  5.3 0.9 %collective-permute-done = f32[32,512]{1,0:T(8,128)S(1)} collective-permute-done((f32[32,512]{1,0:T(8,128)S(1)}, f32[32,512]{1,0:T(8,128)S(1)}, u32[]{:S(2)}, u32[]{:S(2)}) %collective-permute-start) | collective-permute-done | bytes 65568 | tf_op jit(solution)/shard_map/ppermute | solution.py:234
  6.2 5.0 %collective-permute-start.1 = (f32[32,512]{1,0:T(8,128)S(1)}, f32[32,512]{1,0:T(8,128)S(1)}, u32[]{:S(2)}, u32[]{:S(2)}) collective-permute-start(f32[32,512]{1,0:T(8,128)S(1)} %select_add_fusion.2), channel_id=1, source_target_pairs={{0,12},{1,13},{2,14},{3,15},{4,8},{5,9},{6,10},{7,11},{8,4},{9,5},... | collective-permute-start | bytes 196616 | tf_op jit(solution)/shard_map/ppermute | solution.py:234
  11.2 1.3 %collective-permute-start.2 = (f32[32,512]{1,0:T(8,128)S(1)}, f32[32,512]{1,0:T(8,128)S(1)}, u32[]{:S(2)}, u32[]{:S(2)}) collective-permute-start(f32[32,512]{1,0:T(8,128)S(1)} %select_add_fusion.2), channel_id=1, source_target_pairs={{0,8},{1,9},{2,10},{3,11},{4,12},{5,13},{6,14},{7,15},{16,24},{17,... | collective-permute-start | bytes 196616 | tf_op jit(solution)/shard_map/ppermute | solution.py:237
  12.5 1.2 %collective-permute-start.3 = (f32[32,512]{1,0:T(8,128)S(1)}, f32[32,512]{1,0:T(8,128)S(1)}, u32[]{:S(2)}, u32[]{:S(2)}) collective-permute-start(f32[32,512]{1,0:T(8,128)S(1)} %select_add_fusion.2), channel_id=1, source_target_pairs={{0,4},{1,5},{2,6},{3,7},{4,0},{5,1},{6,2},{7,3},{8,12},{9,13},{10,... | collective-permute-start | bytes 196616 | tf_op jit(solution)/shard_map/ppermute | solution.py:234
  13.8 0.7 %collective-permute-start.5 = (f32[2,32,512]{2,1,0:T(8,128)S(1)}, f32[2,32,512]{2,1,0:T(8,128)S(1)}, u32[]{:S(2)}, u32[]{:S(2)}) collective-permute-start(f32[2,32,512]{2,1,0:T(8,128)S(1)} %maximum_select_fusion), channel_id=1, source_target_pairs={{1,8},{3,10},{5,12},{7,14},{17,24},{19,26},{21,28},{23,30}} | collective-permute-start | bytes 393224 | tf_op jit(solution)/shard_map/ppermute | solution.py:246
  14.5 0.0 collective-permute-done.1
  14.5 0.5 %collective-permute-done.2 = f32[32,512]{1,0:T(8,128)S(1)} collective-permute-done((f32[32,512]{1,0:T(8,128)S(1)}, f32[32,512]{1,0:T(8,128)S(1)}, u32[]{:S(2)}, u32[]{:S(2)}) %collective-permute-start.2) | collective-permute-done | bytes 65568 | tf_op jit(solution)/shard_map/ppermute | solution.py:237
  15.0 1.9 %collective-permute-done.3 = f32[32,512]{1,0:T(8,128)S(1)} collective-permute-done((f32[32,512]{1,0:T(8,128)S(1)}, f32[32,512]{1,0:T(8,128)S(1)}, u32[]{:S(2)}, u32[]{:S(2)}) %collective-permute-start.3) | collective-permute-done | bytes 65568 | tf_op jit(solution)/shard_map/ppermute | solution.py:234
  16.9 1.6 %collective-permute-start.4 = (f32[2,32,512]{2,1,0:T(8,128)S(1)}, f32[2,32,512]{2,1,0:T(8,128)S(1)}, u32[]{:S(2)}, u32[]{:S(2)}) collective-permute-start(f32[2,32,512]{2,1,0:T(8,128)S(1)} %pad_maximum_fusion), channel_id=1, source_target_pairs={{0,2},{1,3},{2,0},{3,1},{4,6},{5,7},{6,4},{7,5},{8,10},{9,11},{10,... | collective-permute-start | bytes 393224 | tf_op jit(solution)/shard_map/ppermute | solution.py:234
  18.6 0.0 collective-permute-done.5
  18.6 3.3 %collective-permute-done.4 = f32[2,32,512]{2,1,0:T(8,128)S(1)} collective-permute-done((f32[2,32,512]{2,1,0:T(8,128)S(1)}, f32[2,32,512]{2,1,0:T(8,128)S(1)}, u32[]{:S(2)}, u32[]{:S(2)}) %collective-permute-start.4) | collective-permute-done | bytes 131104 | tf_op jit(solution)/shard_map/ppermute | solution.py:234
  22.0 0.1 collective-permute-start.6
  22.1 1.3 %collective-permute-done.6 = f32[2,32,512]{2,1,0:T(8,128)S(1)} collective-permute-done((f32[2,32,512]{2,1,0:T(8,128)S(1)}, f32[2,32,512]{2,1,0:T(8,128)S(1)}, u32[]{:S(2)}, u32[]{:S(2)}) %collective-permute-start.6) | collective-permute-done | bytes 131104 | tf_op jit(solution)/shard_map/ppermute | solution.py:234
  23.5 0.7 %maximum_bitcast_fusion = (f32[1,2,32,512]{3,2,1,0:T(8,128)}, f32[1,2,32,512]{3,2,1,0:T(8,128)}) fusion(f32[1,32,512]{2,1,0:T(8,128)S(1)} %get-tuple-element.24, f32[1,32,512]{2,1,0:T(8,128)S(1)} %get-tuple-element.23, f32[1,32,512]{2,1,0:T(8,128)S(1)} %get-tuple-element.25, f32[1,32,512]{2,1,0:T(8,128)S(1)} %get-tuple-element.22), kind=kLoop, calls=%fused_computation.4 | loop fusion | flops 65536 | bytes 524288 | tf_op jit(solution)/shard_map/broadcast_in_dim | solution.py:291
  (8 shorter events, 0.2 us)
Async XLA Ops:
  4.8 1.4 %collective-permute-start = (f32[32,512]{1,0:T(8,128)S(1)}, f32[32,512]{1,0:T(8,128)S(1)}, u32[]{:S(2)}, u32[]{:S(2)}) collective-permute-start(f32[32,512]{1,0:T(8,128)S(1)} %get-tuple-element.6), channel_id=1, source_target_pairs={{0,1},{1,0},{2,3},{3,2},{4,5},{5,4},{6,7},{7,6},{8,9},{9,8},{10,11... | collective-permute-start | bytes 196616 | tf_op jit(solution)/shard_map/ppermute | solution.py:234
  6.2 8.3 %collective-permute-start.1 = (f32[32,512]{1,0:T(8,128)S(1)}, f32[32,512]{1,0:T(8,128)S(1)}, u32[]{:S(2)}, u32[]{:S(2)}) collective-permute-start(f32[32,512]{1,0:T(8,128)S(1)} %select_add_fusion.2), channel_id=1, source_target_pairs={{0,12},{1,13},{2,14},{3,15},{4,8},{5,9},{6,10},{7,11},{8,4},{9,5},... | collective-permute-start | bytes 196616 | tf_op jit(solution)/shard_map/ppermute | solution.py:234
  11.2 3.8 %collective-permute-start.2 = (f32[32,512]{1,0:T(8,128)S(1)}, f32[32,512]{1,0:T(8,128)S(1)}, u32[]{:S(2)}, u32[]{:S(2)}) collective-permute-start(f32[32,512]{1,0:T(8,128)S(1)} %select_add_fusion.2), channel_id=1, source_target_pairs={{0,8},{1,9},{2,10},{3,11},{4,12},{5,13},{6,14},{7,15},{16,24},{17,... | collective-permute-start | bytes 196616 | tf_op jit(solution)/shard_map/ppermute | solution.py:237
  12.5 4.3 %collective-permute-start.3 = (f32[32,512]{1,0:T(8,128)S(1)}, f32[32,512]{1,0:T(8,128)S(1)}, u32[]{:S(2)}, u32[]{:S(2)}) collective-permute-start(f32[32,512]{1,0:T(8,128)S(1)} %select_add_fusion.2), channel_id=1, source_target_pairs={{0,4},{1,5},{2,6},{3,7},{4,0},{5,1},{6,2},{7,3},{8,12},{9,13},{10,... | collective-permute-start | bytes 196616 | tf_op jit(solution)/shard_map/ppermute | solution.py:234
  13.8 4.8 %collective-permute-start.5 = (f32[2,32,512]{2,1,0:T(8,128)S(1)}, f32[2,32,512]{2,1,0:T(8,128)S(1)}, u32[]{:S(2)}, u32[]{:S(2)}) collective-permute-start(f32[2,32,512]{2,1,0:T(8,128)S(1)} %maximum_select_fusion), channel_id=1, source_target_pairs={{1,8},{3,10},{5,12},{7,14},{17,24},{19,26},{21,28},{23,30}} | collective-permute-start | bytes 393224 | tf_op jit(solution)/shard_map/ppermute | solution.py:246
  16.9 5.0 %collective-permute-start.4 = (f32[2,32,512]{2,1,0:T(8,128)S(1)}, f32[2,32,512]{2,1,0:T(8,128)S(1)}, u32[]{:S(2)}, u32[]{:S(2)}) collective-permute-start(f32[2,32,512]{2,1,0:T(8,128)S(1)} %pad_maximum_fusion), channel_id=1, source_target_pairs={{0,2},{1,3},{2,0},{3,1},{4,6},{5,7},{6,4},{7,5},{8,10},{9,11},{10,... | collective-permute-start | bytes 393224 | tf_op jit(solution)/shard_map/ppermute | solution.py:234
  22.0 1.4 %collective-permute-start.6 = (f32[2,32,512]{2,1,0:T(8,128)S(1)}, f32[2,32,512]{2,1,0:T(8,128)S(1)}, u32[]{:S(2)}, u32[]{:S(2)}) collective-permute-start(f32[2,32,512]{2,1,0:T(8,128)S(1)} %fusion.1), channel_id=1, source_target_pairs={{0,1},{1,0},{2,3},{3,2},{4,5},{5,4},{6,7},{7,6},{8,9},{9,8},{10,11... | collective-permute-start | bytes 393224 | tf_op jit(solution)/shard_map/ppermute | solution.py:234
